TPU v7x, 32 devices: a whole 2x2x4 slice. The times are simulated.
32 devices in a mesh: grp: 2 (over x), feed: 16 (over z, y, core).
Axes of the slice: x: 2, y: 2, z: 4, core: 2. Of those that a mesh axis runs over, the one named last changes fastest.
Arguments:
- samples: bfloat16 [32, 256, 65536], P(('grp', 'feed')), parts along dimension 0, may hold values from -6 to 6
- pfb_taps: float32 [4, 8192], replicated, may hold values from -0.03125 to 0.03125
Outputs:
- visibility: float32 [16384, 4096], P(('grp', 'feed')), parts along dimension 0
There are 2 independent parts, one for each index of `grp`. A program takes and returns all parts, laid end to end along the dimension named above; an argument that names none is the same for every part. Nothing has to cross between parts.
All inputs are finite; a program needn't handle non-finite values.
Results may differ from a plain program's by a relative error of at most 0.004.
Values may be sent and summed in bfloat16 or wider, within the bound.
No kernel may reach another device: no remote copies, remote signals or barrier semaphores. Data moves between devices by JAX's collectives and lax.ppermute only.
A program may use at most 192 MiB of HBM per device.

v0:
```python
import functools
import math

import jax
import jax.numpy as jnp
import numpy as np
from jax import lax
from jax.experimental import pallas as pl
from jax.experimental.pallas import tpu as pltpu
from jax.sharding import PartitionSpec as P

FIRST_CH = 1536
TIME_BLOCKS = 2
ROWS_DEV = 512
CORES = 2
DEPTH = 1024
BLOCK_ROWS = 64


def dft_rows(fft_len, first_channel, channel_count):
    sample_ids = np.arange(fft_len, dtype=np.int64)
    channel_ids = first_channel + np.arange(channel_count, dtype=np.int64)
    phase = channel_ids[:, None] * sample_ids[None, :] % fft_len
    angle = phase.astype(np.float64) * (2.0 * math.pi / fft_len)
    return np.concatenate([np.cos(angle), -np.sin(angle)], axis=0).astype(np.float32)


def spectra_kernel(
    owners, x_hbm, taps_ref, dft_ref, out_ref, x_buf, table, total, parts, sems
):
    tap_count, fft_len = taps_ref.shape
    columns = dft_ref.shape[0]
    channels = columns // 2
    feed_count = x_hbm.shape[1]
    frame_count = x_hbm.shape[2] // fft_len
    edge = tap_count - 1
    width = tap_count * columns
    later_block = lax.axis_index("feed") >= channels * owners // TIME_BLOCKS

    def fetch(index):
        piece, frame = index // frame_count, lax.rem(index, frame_count)
        source = pl.ds(pl.multiple_of(frame * fft_len + piece * DEPTH, DEPTH), DEPTH)
        rows = pl.ds(pl.multiple_of(frame * feed_count, feed_count), feed_count)
        span = pl.ds(pl.multiple_of(piece * DEPTH, DEPTH), DEPTH)
        return pltpu.make_async_copy(x_hbm.at[0, :, source], x_buf.at[rows, span], sems.at[index])

    @pl.loop(0, frame_count * fft_len // DEPTH)
    def _(index):
        fetch(index).start()

    total[...] = jnp.zeros_like(total)

    @pl.loop(0, fft_len // DEPTH)
    def _(index):
        span = pl.ds(pl.multiple_of(index * DEPTH, DEPTH), DEPTH)
        dft = dft_ref[:, span]
        scaled = jnp.concatenate([taps_ref[m : m + 1, span] * dft for m in range(tap_count)], axis=0)
        high = scaled.astype(jnp.bfloat16).astype(jnp.float32)
        both = jnp.concatenate([high, scaled - high], axis=0)
        table[span, :] = both.T.astype(jnp.bfloat16)

    @pl.loop(0, fft_len // DEPTH)
    def _(piece):
        @pl.loop(0, frame_count)
        def _(frame):
            fetch(piece * frame_count + frame).wait()

        span = pl.ds(pl.multiple_of(piece * DEPTH, DEPTH), DEPTH)
        total[...] += jnp.dot(x_buf[:, span], table[span, :], preferred_element_type=jnp.float32)

    window = [None] * (frame_count + edge)
    for frame in range(frame_count):
        turned = total[frame * feed_count : (frame + 1) * feed_count].T
        summed = turned[:width] + turned[width:]
        for m in range(tap_count):
            term = summed[m * columns : (m + 1) * columns]
            spot = frame + edge - m
            window[spot] = term if window[spot] is None else window[spot] + term
    for spot in range(frame_count + edge):
        parts[:, spot, :] = window[spot]

    copies = out_ref.shape[0] // channels
    for c in range(channels):
        now = jnp.concatenate([parts[c, :frame_count], parts[channels + c, :frame_count]], axis=0)
        high = now.astype(jnp.bfloat16)
        low = now - high.astype(jnp.float32)
        low = jnp.concatenate([low[:4], low[frame_count : frame_count + 4]], axis=0)
        tail = jnp.concatenate(
            [parts[c, frame_count : frame_count + 4], parts[channels + c, frame_count : frame_count + 4]],
            axis=0,
        )
        sublane = lax.broadcasted_iota(jnp.int32, tail.shape, 0)
        tail = jnp.where(sublane % 4 < edge, tail, 0.0)
        tail_high = tail.astype(jnp.bfloat16).astype(jnp.float32)
        tail_low = tail - tail_high
        extra = jnp.concatenate(
            [jnp.where(later_block, low, tail_high), jnp.where(later_block, 0.0, tail_low)], axis=0
        ).astype(jnp.bfloat16)
        whole = jnp.concatenate([high, extra], axis=0)
        for o in range(copies):
            out_ref[c * copies + o] = whole


def correlate_kernel(
    scale, owners, own_ref, other_ref, out_hbm, right, left, out_buf, sems
):
    lines, rows, feed_count = own_ref.shape
    group_span = lines * CORES // TIME_BLOCKS
    frame_count = rows // 4
    total_feeds = right.shape[1]
    blocks = left.shape[0]
    block_rows = left.shape[1] // 2
    my_index = lax.axis_index("feed")
    my_core = my_index % CORES

    def arrived(device):
        mine, core = device // CORES, device % CORES
        return jnp.where(my_core == core, own_ref[mine], other_ref[mine])

    for g in range(group_span):
        span = slice(g * feed_count, (g + 1) * feed_count)
        low, high = arrived(g), arrived(group_span + g)
        first = low.astype(jnp.float32)
        second = high.astype(jnp.float32)
        extra = (
            first[2 * frame_count : 3 * frame_count]
            + first[3 * frame_count :]
            + second[2 * frame_count : 3 * frame_count]
        )
        zero = jnp.zeros((frame_count - 4, feed_count), jnp.float32)
        extra = jnp.concatenate([extra[:4], zero, extra[4:8], zero], axis=0)
        fixed = second[: 2 * frame_count] + extra
        right[: 2 * frame_count, span] = low[: 2 * frame_count]
        right[2 * frame_count :, span] = fixed.astype(jnp.bfloat16)
    row_start = my_index % owners * ROWS_DEV
    mine = right[:, pl.ds(pl.multiple_of(row_start, ROWS_DEV), ROWS_DEV)].astype(jnp.float32)
    halves = [mine[k * frame_count : (k + 1) * frame_count] for k in range(4)]
    swapped = jnp.concatenate([halves[1], -halves[0], halves[3], -halves[2]], axis=0)
    left[:, :block_rows, :] = mine.T.astype(jnp.bfloat16).reshape(blocks, block_rows, rows)
    left[:, block_rows:, :] = swapped.T.astype(jnp.bfloat16).reshape(blocks, block_rows, rows)

    def store(block):
        span = pl.ds(pl.multiple_of(block * block_rows, block_rows), block_rows)
        return pltpu.make_async_copy(out_buf.at[span], out_hbm.at[span], sems.at[block])

    @pl.loop(0, blocks)
    def _(block):
        product = jnp.dot(left[block], right[...], preferred_element_type=jnp.float32) * scale
        span = pl.ds(pl.multiple_of(block * block_rows, block_rows), block_rows)
        out_buf[span, :total_feeds] = product[:block_rows]
        out_buf[span, total_feeds:] = product[block_rows:]
        store(block).start()

    @pl.loop(0, blocks)
    def _(block):
        store(block).wait()


def body(samples, pfb_taps):
    feed_count = samples.shape[1]
    tap_count, fft_len = pfb_taps.shape
    frame_count = samples.shape[2] // fft_len
    devices = lax.axis_size("feed")
    total_feeds = feed_count * devices // TIME_BLOCKS
    channels = devices * ROWS_DEV // total_feeds
    owners = total_feeds // ROWS_DEV
    spectra_count = TIME_BLOCKS * frame_count
    columns = 2 * channels
    rows = 4 * frame_count
    lines = devices // CORES
    dft = jnp.asarray(dft_rows(fft_len, FIRST_CH, channels))
    in_vmem = pl.BlockSpec(memory_space=pltpu.VMEM)
    outgoing = pl.pallas_call(
        functools.partial(spectra_kernel, owners),
        out_shape=jax.ShapeDtypeStruct((lines, rows, feed_count), jnp.bfloat16),
        in_specs=[pl.BlockSpec(memory_space=pl.ANY), in_vmem, in_vmem],
        out_specs=in_vmem,
        scratch_shapes=[
            pltpu.VMEM((frame_count * feed_count, fft_len), jnp.bfloat16),
            pltpu.VMEM((fft_len, 2 * tap_count * columns), jnp.bfloat16),
            pltpu.VMEM((frame_count * feed_count, 2 * tap_count * columns), jnp.float32),
            pltpu.VMEM((columns, 2 * frame_count, feed_count), jnp.float32),
            pltpu.SemaphoreType.DMA((frame_count * fft_len // DEPTH,)),
        ],
        compiler_params=pltpu.CompilerParams(vmem_limit_bytes=56 * 2**20),
        name="spectra",
    )(samples, pfb_taps, dft)
    same_core = [[line * CORES + core for line in range(lines)] for core in range(CORES)]
    own = lax.all_to_all(outgoing, "feed", 0, 0, axis_index_groups=same_core, tiled=True)
    other = lax.ppermute(own, "feed", [(d, d ^ 1) for d in range(devices)])
    blocks = ROWS_DEV // BLOCK_ROWS
    return pl.pallas_call(
        functools.partial(correlate_kernel, 1.0 / spectra_count, owners),
        out_shape=jax.ShapeDtypeStruct((ROWS_DEV, 2 * total_feeds), jnp.float32),
        in_specs=[in_vmem, in_vmem],
        out_specs=pl.BlockSpec(memory_space=pl.ANY),
        scratch_shapes=[
            pltpu.VMEM((rows, total_feeds), jnp.bfloat16),
            pltpu.VMEM((blocks, 2 * BLOCK_ROWS, rows), jnp.bfloat16),
            pltpu.VMEM((ROWS_DEV, 2 * total_feeds), jnp.float32),
            pltpu.SemaphoreType.DMA((blocks,)),
        ],
        compiler_params=pltpu.CompilerParams(vmem_limit_bytes=32 * 2**20),
        name="correlate",
    )(own, other)


def solution(mesh):
    placed = (P(("grp", "feed"), None, None), P())
    return jax.shard_map(
        body, mesh=mesh, in_specs=placed, out_specs=P(("grp", "feed"), None), check_vma=False
    )
```

profile of v0, /device:TPU:0, one launch (start us, length us, event | category | flops | bytes accessed | tf_op | source)
XLA Modules:
  0.0 35.0 jit_solution(9516721364260822794)
XLA Ops:
  0.0 15.2 %spectra.1 = bf16[8,32,256]{2,1,0:T(8,128)(2,1)} custom-call(bf16[1,256,65536]{2,1,0:T(8,128)(2,1)} %x_hbm.1, f32[4,8192]{1,0:T(4,128)} %taps_ref.1, f32[8,8192]{1,0:T(8,128)} %constant.2.clone.dft_ref), custom_call_target="tpu_custom_call" | custom-call | tf_op jit(solution)/shard_map/spectra/pallas_call | solution.py:173
  15.2 14.6 %all_to_all.5.own_ref = bf16[8,32,256]{2,1,0:T(8,128)(2,1)S(1)} all-to-all(bf16[8,32,256]{2,1,0:T(8,128)(2,1)} %spectra.1), channel_id=1, replica_groups={{0,2,4,6,8,10,12,14},{1,3,5,7,9,11,13,15},{16,18,20,22,24,26,28,30},{17..., dimensions={0} | all-to-all | bytes 262144 | tf_op jit(solution)/shard_map/all_to_all | solution.py:189
  29.8 0.0 collective-permute-start
  29.8 1.3 %collective-permute-done.other_ref = bf16[8,32,256]{2,1,0:T(8,128)(2,1)S(1)} collective-permute-done((bf16[8,32,256]{2,1,0:T(8,128)(2,1)S(1)}, bf16[8,32,256]{2,1,0:T(8,128)(2,1)S(1)}, u32[]{:S(2)}, u32[]{:S(2)}) %collective-permute-start) | collective-permute-done | bytes 131104 | tf_op jit(solution)/shard_map/ppermute | solution.py:190
  31.2 3.8 %correlate.1 = f32[512,4096]{1,0:T(8,128)} custom-call(bf16[8,32,256]{2,1,0:T(8,128)(2,1)S(1)} %all_to_all.5.own_ref, bf16[8,32,256]{2,1,0:T(8,128)(2,1)S(1)} %collective-permute-done.other_ref), custom_call_target="tpu_custom_call" | custom-call | tf_op jit(solution)/shard_map/correlate/pallas_call | solution.py:192
Async XLA Ops:
  29.8 1.3 %collective-permute-start = (bf16[8,32,256]{2,1,0:T(8,128)(2,1)S(1)}, bf16[8,32,256]{2,1,0:T(8,128)(2,1)S(1)}, u32[]{:S(2)}, u32[]{:S(2)}) collective-permute-start(bf16[8,32,256]{2,1,0:T(8,128)(2,1)S(1)} %all_to_all.5.own_ref), channel_id=1, source_target_pairs={{0,1},{1,0},{2,3},{3,2},{4,5},{5,4},{6,7},{7,6},{8,9},{9,8},{10,11... | collective-permute-start | bytes 393224 | tf_op jit(solution)/shard_map/ppermute | solution.py:190
where the time goes:
time: 35.2 us; the launch traced here: 35 us
  Pallas kernels  19 us (54%)
  blocking collectives  14.6 us (41%)
  waiting for transfers between devices  1.35 us (4%)
    pallas_call x1, Pallas kernels, body(): pl.pallas_call(functools.partial(spectra_kernel, owners), out_shape=jax.S...  15.2 us
    all_to_all x1, blocking collectives, body(): lax.all_to_all(outgoing, 'feed', 0, 0, axis_index_groups=same_core, tiled...  14.6 us
    pallas_call x1, Pallas kernels, body(): pl.pallas_call(functools.partial(correlate_kernel, 1.0 / spectra_count, o...  3.81 us
    ppermute x1, waiting for transfers between devices, body(): other = lax.ppermute(own, 'feed', [(d, d ^ 1) for d in range(devices)])  1.35 us
  transfers between devices with their start and end apart: 1, of which 1 were waited for; matrix products, arithmetic and copies ran while one was open for 0% of the time, Pallas kernels for 0%

commit v1 on v0

--- a/solution.py
+++ b/solution.py
@@ -13,7 +13,8 @@
 TIME_BLOCKS = 2
 ROWS_DEV = 512
 CORES = 2
-DEPTH = 1024
+PIECES = 4
+TABLE_STEP = 1024
 BLOCK_ROWS = 64
 
 
@@ -26,56 +27,83 @@
 
 
 def spectra_kernel(
-    owners, x_hbm, taps_ref, dft_ref, out_ref, x_buf, table, total, parts, sems
+    owners, x_hbm, taps_hbm, dft_hbm, out_ref,
+    taps_ref, dft_ref, x_buf, table, raw, window, parts, small_sems, sems,
 ):
     tap_count, fft_len = taps_ref.shape
     columns = dft_ref.shape[0]
     channels = columns // 2
-    feed_count = x_hbm.shape[1]
     frame_count = x_hbm.shape[2] // fft_len
+    piece = fft_len // PIECES
     edge = tap_count - 1
     width = tap_count * columns
     later_block = lax.axis_index("feed") >= channels * owners // TIME_BLOCKS
 
+    small = [
+        pltpu.make_async_copy(taps_hbm, taps_ref, small_sems.at[0]),
+        pltpu.make_async_copy(dft_hbm, dft_ref, small_sems.at[1]),
+    ]
+    for copy in small:
+        copy.start()
+
     def fetch(index):
-        piece, frame = index // frame_count, lax.rem(index, frame_count)
-        source = pl.ds(pl.multiple_of(frame * fft_len + piece * DEPTH, DEPTH), DEPTH)
-        rows = pl.ds(pl.multiple_of(frame * feed_count, feed_count), feed_count)
-        span = pl.ds(pl.multiple_of(piece * DEPTH, DEPTH), DEPTH)
-        return pltpu.make_async_copy(x_hbm.at[0, :, source], x_buf.at[rows, span], sems.at[index])
-
-    @pl.loop(0, frame_count * fft_len // DEPTH)
+        span = pl.ds(pl.multiple_of(index * piece, piece), piece)
+        return pltpu.make_async_copy(x_hbm.at[0, :, span], x_buf.at[:, span], sems.at[index])
+
+    @pl.loop(0, frame_count * PIECES)
     def _(index):
         fetch(index).start()
 
-    total[...] = jnp.zeros_like(total)
-
-    @pl.loop(0, fft_len // DEPTH)
+    window[...] = jnp.zeros_like(window)
+    raw[...] = jnp.zeros_like(raw)
+    for copy in small:
+        copy.wait()
+
+    @pl.loop(0, fft_len // TABLE_STEP)
     def _(index):
-        span = pl.ds(pl.multiple_of(index * DEPTH, DEPTH), DEPTH)
+        span = pl.ds(pl.multiple_of(index * TABLE_STEP, TABLE_STEP), TABLE_STEP)
         dft = dft_ref[:, span]
         scaled = jnp.concatenate([taps_ref[m : m + 1, span] * dft for m in range(tap_count)], axis=0)
         high = scaled.astype(jnp.bfloat16).astype(jnp.float32)
         both = jnp.concatenate([high, scaled - high], axis=0)
         table[span, :] = both.T.astype(jnp.bfloat16)
 
-    @pl.loop(0, fft_len // DEPTH)
-    def _(piece):
-        @pl.loop(0, frame_count)
-        def _(frame):
-            fetch(piece * frame_count + frame).wait()
-
-        span = pl.ds(pl.multiple_of(piece * DEPTH, DEPTH), DEPTH)
-        total[...] += jnp.dot(x_buf[:, span], table[span, :], preferred_element_type=jnp.float32)
-
-    window = [None] * (frame_count + edge)
-    for frame in range(frame_count):
-        turned = total[frame * feed_count : (frame + 1) * feed_count].T
+    def fold(frame, total):
+        turned = total.T
         summed = turned[:width] + turned[width:]
         for m in range(tap_count):
-            term = summed[m * columns : (m + 1) * columns]
-            spot = frame + edge - m
-            window[spot] = term if window[spot] is None else window[spot] + term
+            window[frame + edge - m] += summed[m * columns : (m + 1) * columns]
+
+    def two_dots(frame, begin, depth):
+        total = None
+        for offset in (begin, begin + depth):
+            start = pl.multiple_of(frame * fft_len + offset, depth)
+            product = jnp.dot(
+                x_buf[:, pl.ds(start, depth)],
+                table[offset : offset + depth, :],
+                preferred_element_type=jnp.float32,
+            )
+            total = product if total is None else total + product
+        return total
+
+    @pl.loop(0, frame_count - 1)
+    def _(frame):
+        for p in range(PIECES):
+            fetch(frame * PIECES + p).wait()
+        fold(jnp.maximum(frame - 1, 0), raw[...])
+        raw[...] = two_dots(frame, 0, fft_len // 2)
+
+    last = frame_count - 1
+    total = None
+    for p in range(0, PIECES, 2):
+        for k in (p, p + 1):
+            fetch(last * PIECES + k).wait()
+        if p == 0:
+            fold(last - 1, raw[...])
+        product = two_dots(last, p * piece, piece)
+        total = product if total is None else total + product
+    fold(last, total)
+
     for spot in range(frame_count + edge):
         parts[:, spot, :] = window[spot]
 
@@ -173,14 +201,18 @@
     outgoing = pl.pallas_call(
         functools.partial(spectra_kernel, owners),
         out_shape=jax.ShapeDtypeStruct((lines, rows, feed_count), jnp.bfloat16),
-        in_specs=[pl.BlockSpec(memory_space=pl.ANY), in_vmem, in_vmem],
+        in_specs=[pl.BlockSpec(memory_space=pl.ANY)] * 3,
         out_specs=in_vmem,
         scratch_shapes=[
-            pltpu.VMEM((frame_count * feed_count, fft_len), jnp.bfloat16),
+            pltpu.VMEM(pfb_taps.shape, jnp.float32),
+            pltpu.VMEM(dft.shape, jnp.float32),
+            pltpu.VMEM((feed_count, samples.shape[2]), jnp.bfloat16),
             pltpu.VMEM((fft_len, 2 * tap_count * columns), jnp.bfloat16),
-            pltpu.VMEM((frame_count * feed_count, 2 * tap_count * columns), jnp.float32),
+            pltpu.VMEM((feed_count, 2 * tap_count * columns), jnp.float32),
+            pltpu.VMEM((frame_count + tap_count - 1, columns, feed_count), jnp.float32),
             pltpu.VMEM((columns, 2 * frame_count, feed_count), jnp.float32),
-            pltpu.SemaphoreType.DMA((frame_count * fft_len // DEPTH,)),
+            pltpu.SemaphoreType.DMA((2,)),
+            pltpu.SemaphoreType.DMA((frame_count * PIECES,)),
         ],
         compiler_params=pltpu.CompilerParams(vmem_limit_bytes=56 * 2**20),
         name="spectra",

time: 35.2 us -> 33.6 us (0.955)
  Pallas kernels: 19 us -> 17.3 us
    pallas_call x1, Pallas kernels: 15.2 us -> 13.5 us  [body(): pl.pallas_call(functools.partial(spectra_kernel, owners), out_shape=jax.S...]
where the time goes in v1:
time: 33.6 us; the launch traced here: 33.3 us
  Pallas kernels  17.3 us (51%)
  blocking collectives  14.6 us (43%)
  waiting for transfers between devices  1.35 us (4%)
    all_to_all x1, blocking collectives, body(): lax.all_to_all(outgoing, 'feed', 0, 0, axis_index_groups=same_core, tiled...  14.6 us
    pallas_call x1, Pallas kernels, body(): pl.pallas_call(functools.partial(spectra_kernel, owners), out_shape=jax.S...  13.5 us
    pallas_call x1, Pallas kernels, body(): pl.pallas_call(functools.partial(correlate_kernel, 1.0 / spectra_count, o...  3.82 us
    ppermute x1, waiting for transfers between devices, body(): other = lax.ppermute(own, 'feed', [(d, d ^ 1) for d in range(devices)])  1.35 us
  transfers between devices with their start and end apart: 1, of which 1 were waited for; matrix products, arithmetic and copies ran while one was open for 0% of the time, Pallas kernels for 0%

profile of v1, /device:TPU:0, one launch (start us, length us, event | category | flops | bytes accessed | tf_op | source)
XLA Modules:
  0.0 33.3 jit_solution(7530921946956405231)
XLA Ops:
  0.0 13.5 %spectra.1 = bf16[8,32,256]{2,1,0:T(8,128)(2,1)} custom-call(bf16[1,256,65536]{2,1,0:T(8,128)(2,1)} %x_hbm.1, f32[4,8192]{1,0:T(4,128)} %taps_hbm.1, f32[8,8192]{1,0:T(8,128)} %constant.2.clone.dft_hbm), custom_call_target="tpu_custom_call" | custom-call | tf_op jit(solution)/shard_map/spectra/pallas_call | solution.py:201
  13.5 14.6 %all_to_all.5.own_ref = bf16[8,32,256]{2,1,0:T(8,128)(2,1)S(1)} all-to-all(bf16[8,32,256]{2,1,0:T(8,128)(2,1)} %spectra.1), channel_id=1, replica_groups={{0,2,4,6,8,10,12,14},{1,3,5,7,9,11,13,15},{16,18,20,22,24,26,28,30},{17..., dimensions={0} | all-to-all | bytes 262144 | tf_op jit(solution)/shard_map/all_to_all | solution.py:221
  28.2 0.0 collective-permute-start
  28.2 1.3 %collective-permute-done.other_ref = bf16[8,32,256]{2,1,0:T(8,128)(2,1)S(1)} collective-permute-done((bf16[8,32,256]{2,1,0:T(8,128)(2,1)S(1)}, bf16[8,32,256]{2,1,0:T(8,128)(2,1)S(1)}, u32[]{:S(2)}, u32[]{:S(2)}) %collective-permute-start) | collective-permute-done | bytes 131104 | tf_op jit(solution)/shard_map/ppermute | solution.py:222
  29.5 3.8 %correlate.1 = f32[512,4096]{1,0:T(8,128)} custom-call(bf16[8,32,256]{2,1,0:T(8,128)(2,1)S(1)} %all_to_all.5.own_ref, bf16[8,32,256]{2,1,0:T(8,128)(2,1)S(1)} %collective-permute-done.other_ref), custom_call_target="tpu_custom_call" | custom-call | tf_op jit(solution)/shard_map/correlate/pallas_call | solution.py:224
Async XLA Ops:
  28.2 1.3 %collective-permute-start = (bf16[8,32,256]{2,1,0:T(8,128)(2,1)S(1)}, bf16[8,32,256]{2,1,0:T(8,128)(2,1)S(1)}, u32[]{:S(2)}, u32[]{:S(2)}) collective-permute-start(bf16[8,32,256]{2,1,0:T(8,128)(2,1)S(1)} %all_to_all.5.own_ref), channel_id=1, source_target_pairs={{0,1},{1,0},{2,3},{3,2},{4,5},{5,4},{6,7},{7,6},{8,9},{9,8},{10,11... | collective-permute-start | bytes 393224 | tf_op jit(solution)/shard_map/ppermute | solution.py:222

commit v2 on v1

--- a/solution.py
+++ b/solution.py
@@ -74,24 +74,27 @@
         for m in range(tap_count):
             window[frame + edge - m] += summed[m * columns : (m + 1) * columns]
 
-    def two_dots(frame, begin, depth):
-        total = None
-        for offset in (begin, begin + depth):
+    def dots(frame, begin, depth, count):
+        terms = []
+        for offset in range(begin, begin + count * depth, depth):
             start = pl.multiple_of(frame * fft_len + offset, depth)
-            product = jnp.dot(
-                x_buf[:, pl.ds(start, depth)],
-                table[offset : offset + depth, :],
-                preferred_element_type=jnp.float32,
+            terms.append(
+                jnp.dot(
+                    x_buf[:, pl.ds(start, depth)],
+                    table[offset : offset + depth, :],
+                    preferred_element_type=jnp.float32,
+                )
             )
-            total = product if total is None else total + product
-        return total
+        while len(terms) > 1:
+            terms = [one + two for one, two in zip(terms[::2], terms[1::2])]
+        return terms[0]
 
     @pl.loop(0, frame_count - 1)
     def _(frame):
         for p in range(PIECES):
             fetch(frame * PIECES + p).wait()
         fold(jnp.maximum(frame - 1, 0), raw[...])
-        raw[...] = two_dots(frame, 0, fft_len // 2)
+        raw[...] = dots(frame, 0, fft_len // 4, 4)
 
     last = frame_count - 1
     total = None
@@ -100,7 +103,7 @@
             fetch(last * PIECES + k).wait()
         if p == 0:
             fold(last - 1, raw[...])
-        product = two_dots(last, p * piece, piece)
+        product = dots(last, p * piece, piece, 2)
         total = product if total is None else total + product
     fold(last, total)
 

time: 33.6 us -> 33.6 us (level)
  no operation moved by 1% of the time
where the time goes in v2:
time: 33.6 us; the launch traced here: 33.3 us
  Pallas kernels  17.3 us (51%)
  blocking collectives  14.6 us (43%)
  waiting for transfers between devices  1.35 us (4%)
    all_to_all x1, blocking collectives, body(): lax.all_to_all(outgoing, 'feed', 0, 0, axis_index_groups=same_core, tiled...  14.6 us
    pallas_call x1, Pallas kernels, body(): pl.pallas_call(functools.partial(spectra_kernel, owners), out_shape=jax.S...  13.5 us
    pallas_call x1, Pallas kernels, body(): pl.pallas_call(functools.partial(correlate_kernel, 1.0 / spectra_count, o...  3.82 us
    ppermute x1, waiting for transfers between devices, body(): other = lax.ppermute(own, 'feed', [(d, d ^ 1) for d in range(devices)])  1.35 us
  transfers between devices with their start and end apart: 1, of which 1 were waited for; matrix products, arithmetic and copies ran while one was open for 0% of the time, Pallas kernels for 0%

profile of v2, /device:TPU:0, one launch (start us, length us, event | category | flops | bytes accessed | tf_op | source)
XLA Modules:
  0.0 33.3 jit_solution(3062784622339693492)
XLA Ops:
  0.0 13.5 %spectra.1 = bf16[8,32,256]{2,1,0:T(8,128)(2,1)} custom-call(bf16[1,256,65536]{2,1,0:T(8,128)(2,1)} %x_hbm.1, f32[4,8192]{1,0:T(4,128)} %taps_hbm.1, f32[8,8192]{1,0:T(8,128)} %constant.2.clone.dft_hbm), custom_call_target="tpu_custom_call" | custom-call | tf_op jit(solution)/shard_map/spectra/pallas_call | solution.py:204
  13.5 14.6 %all_to_all.5.own_ref = bf16[8,32,256]{2,1,0:T(8,128)(2,1)S(1)} all-to-all(bf16[8,32,256]{2,1,0:T(8,128)(2,1)} %spectra.1), channel_id=1, replica_groups={{0,2,4,6,8,10,12,14},{1,3,5,7,9,11,13,15},{16,18,20,22,24,26,28,30},{17..., dimensions={0} | all-to-all | bytes 262144 | tf_op jit(solution)/shard_map/all_to_all | solution.py:224
  28.2 0.0 collective-permute-start
  28.2 1.3 %collective-permute-done.other_ref = bf16[8,32,256]{2,1,0:T(8,128)(2,1)S(1)} collective-permute-done((bf16[8,32,256]{2,1,0:T(8,128)(2,1)S(1)}, bf16[8,32,256]{2,1,0:T(8,128)(2,1)S(1)}, u32[]{:S(2)}, u32[]{:S(2)}) %collective-permute-start) | collective-permute-done | bytes 131104 | tf_op jit(solution)/shard_map/ppermute | solution.py:225
  29.5 3.8 %correlate.1 = f32[512,4096]{1,0:T(8,128)} custom-call(bf16[8,32,256]{2,1,0:T(8,128)(2,1)S(1)} %all_to_all.5.own_ref, bf16[8,32,256]{2,1,0:T(8,128)(2,1)S(1)} %collective-permute-done.other_ref), custom_call_target="tpu_custom_call" | custom-call | tf_op jit(solution)/shard_map/correlate/pallas_call | solution.py:227
Async XLA Ops:
  28.2 1.3 %collective-permute-start = (bf16[8,32,256]{2,1,0:T(8,128)(2,1)S(1)}, bf16[8,32,256]{2,1,0:T(8,128)(2,1)S(1)}, u32[]{:S(2)}, u32[]{:S(2)}) collective-permute-start(bf16[8,32,256]{2,1,0:T(8,128)(2,1)S(1)} %all_to_all.5.own_ref), channel_id=1, source_target_pairs={{0,1},{1,0},{2,3},{3,2},{4,5},{5,4},{6,7},{7,6},{8,9},{9,8},{10,11... | collective-permute-start | bytes 393224 | tf_op jit(solution)/shard_map/ppermute | solution.py:225

commit v3 on v1

--- a/solution.py
+++ b/solution.py
@@ -50,9 +50,10 @@
         span = pl.ds(pl.multiple_of(index * piece, piece), piece)
         return pltpu.make_async_copy(x_hbm.at[0, :, span], x_buf.at[:, span], sems.at[index])
 
-    @pl.loop(0, frame_count * PIECES)
-    def _(index):
-        fetch(index).start()
+    @pl.loop(0, frame_count * PIECES // 2)
+    def _(pair):
+        fetch(2 * pair).start(priority=0)
+        fetch(2 * pair + 1).start(priority=1)
 
     window[...] = jnp.zeros_like(window)
     raw[...] = jnp.zeros_like(raw)
@@ -171,13 +172,15 @@
         span = pl.ds(pl.multiple_of(block * block_rows, block_rows), block_rows)
         return pltpu.make_async_copy(out_buf.at[span], out_hbm.at[span], sems.at[block])
 
-    @pl.loop(0, blocks)
-    def _(block):
-        product = jnp.dot(left[block], right[...], preferred_element_type=jnp.float32) * scale
-        span = pl.ds(pl.multiple_of(block * block_rows, block_rows), block_rows)
-        out_buf[span, :total_feeds] = product[:block_rows]
-        out_buf[span, total_feeds:] = product[block_rows:]
-        store(block).start()
+    @pl.loop(0, blocks // 2)
+    def _(pair):
+        for turn in range(2):
+            block = 2 * pair + turn
+            product = jnp.dot(left[block], right[...], preferred_element_type=jnp.float32) * scale
+            span = pl.ds(pl.multiple_of(block * block_rows, block_rows), block_rows)
+            out_buf[span, :total_feeds] = product[:block_rows]
+            out_buf[span, total_feeds:] = product[block_rows:]
+            store(block).start(priority=turn)
 
     @pl.loop(0, blocks)
     def _(block):

time: 33.6 us -> 37.8 us (1.12)
  Pallas kernels: 17.3 us -> 21.6 us
    pallas_call x1, Pallas kernels: 13.5 us -> 17.7 us  [body(): pl.pallas_call(functools.partial(spectra_kernel, owners), out_shape=jax.S...]
where the time goes in v3:
time: 37.8 us; the launch traced here: 37.6 us
  Pallas kernels  21.6 us (57%)
  blocking collectives  14.6 us (39%)
  waiting for transfers between devices  1.35 us (4%)
    pallas_call x1, Pallas kernels, body(): pl.pallas_call(functools.partial(spectra_kernel, owners), out_shape=jax.S...  17.7 us
    all_to_all x1, blocking collectives, body(): lax.all_to_all(outgoing, 'feed', 0, 0, axis_index_groups=same_core, tiled...  14.6 us
    pallas_call x1, Pallas kernels, body(): pl.pallas_call(functools.partial(correlate_kernel, 1.0 / spectra_count, o...  3.82 us
    ppermute x1, waiting for transfers between devices, body(): other = lax.ppermute(own, 'feed', [(d, d ^ 1) for d in range(devices)])  1.35 us
  transfers between devices with their start and end apart: 1, of which 1 were waited for; matrix products, arithmetic and copies ran while one was open for 0% of the time, Pallas kernels for 0%

profile of v3, /device:TPU:0, one launch (start us, length us, event | category | flops | bytes accessed | tf_op | source)
XLA Modules:
  0.0 37.6 jit_solution(7953788840683061709)
XLA Ops:
  0.0 17.7 %spectra.1 = bf16[8,32,256]{2,1,0:T(8,128)(2,1)} custom-call(bf16[1,256,65536]{2,1,0:T(8,128)(2,1)} %x_hbm.1, f32[4,8192]{1,0:T(4,128)} %taps_hbm.1, f32[8,8192]{1,0:T(8,128)} %constant.2.clone.dft_hbm), custom_call_target="tpu_custom_call" | custom-call | tf_op jit(solution)/shard_map/spectra/pallas_call | solution.py:204
  17.8 14.6 %all_to_all.5.own_ref = bf16[8,32,256]{2,1,0:T(8,128)(2,1)S(1)} all-to-all(bf16[8,32,256]{2,1,0:T(8,128)(2,1)} %spectra.1), channel_id=1, replica_groups={{0,2,4,6,8,10,12,14},{1,3,5,7,9,11,13,15},{16,18,20,22,24,26,28,30},{17..., dimensions={0} | all-to-all | bytes 262144 | tf_op jit(solution)/shard_map/all_to_all | solution.py:224
  32.4 0.0 collective-permute-start
  32.4 1.3 %collective-permute-done.other_ref = bf16[8,32,256]{2,1,0:T(8,128)(2,1)S(1)} collective-permute-done((bf16[8,32,256]{2,1,0:T(8,128)(2,1)S(1)}, bf16[8,32,256]{2,1,0:T(8,128)(2,1)S(1)}, u32[]{:S(2)}, u32[]{:S(2)}) %collective-permute-start) | collective-permute-done | bytes 131104 | tf_op jit(solution)/shard_map/ppermute | solution.py:225
  33.7 3.8 %correlate.1 = f32[512,4096]{1,0:T(8,128)} custom-call(bf16[8,32,256]{2,1,0:T(8,128)(2,1)S(1)} %all_to_all.5.own_ref, bf16[8,32,256]{2,1,0:T(8,128)(2,1)S(1)} %collective-permute-done.other_ref), custom_call_target="tpu_custom_call" | custom-call | tf_op jit(solution)/shard_map/correlate/pallas_call | solution.py:227
Async XLA Ops:
  32.4 1.3 %collective-permute-start = (bf16[8,32,256]{2,1,0:T(8,128)(2,1)S(1)}, bf16[8,32,256]{2,1,0:T(8,128)(2,1)S(1)}, u32[]{:S(2)}, u32[]{:S(2)}) collective-permute-start(bf16[8,32,256]{2,1,0:T(8,128)(2,1)S(1)} %all_to_all.5.own_ref), channel_id=1, source_target_pairs={{0,1},{1,0},{2,3},{3,2},{4,5},{5,4},{6,7},{7,6},{8,9},{9,8},{10,11... | collective-permute-start | bytes 393224 | tf_op jit(solution)/shard_map/ppermute | solution.py:225

commit v4 on v1

--- a/solution.py
+++ b/solution.py
@@ -119,11 +119,7 @@
         )
         sublane = lax.broadcasted_iota(jnp.int32, tail.shape, 0)
         tail = jnp.where(sublane % 4 < edge, tail, 0.0)
-        tail_high = tail.astype(jnp.bfloat16).astype(jnp.float32)
-        tail_low = tail - tail_high
-        extra = jnp.concatenate(
-            [jnp.where(later_block, low, tail_high), jnp.where(later_block, 0.0, tail_low)], axis=0
-        ).astype(jnp.bfloat16)
+        extra = jnp.where(later_block, low, tail).astype(jnp.bfloat16)
         whole = jnp.concatenate([high, extra], axis=0)
         for o in range(copies):
             out_ref[c * copies + o] = whole
@@ -134,7 +130,7 @@
 ):
     lines, rows, feed_count = own_ref.shape
     group_span = lines * CORES // TIME_BLOCKS
-    frame_count = rows // 4
+    frame_count = rows // 3
     total_feeds = right.shape[1]
     blocks = left.shape[0]
     block_rows = left.shape[1] // 2
@@ -150,11 +146,7 @@
         low, high = arrived(g), arrived(group_span + g)
         first = low.astype(jnp.float32)
         second = high.astype(jnp.float32)
-        extra = (
-            first[2 * frame_count : 3 * frame_count]
-            + first[3 * frame_count :]
-            + second[2 * frame_count : 3 * frame_count]
-        )
+        extra = first[2 * frame_count :] + second[2 * frame_count :]
         zero = jnp.zeros((frame_count - 4, feed_count), jnp.float32)
         extra = jnp.concatenate([extra[:4], zero, extra[4:8], zero], axis=0)
         fixed = second[: 2 * frame_count] + extra
@@ -164,8 +156,8 @@
     mine = right[:, pl.ds(pl.multiple_of(row_start, ROWS_DEV), ROWS_DEV)].astype(jnp.float32)
     halves = [mine[k * frame_count : (k + 1) * frame_count] for k in range(4)]
     swapped = jnp.concatenate([halves[1], -halves[0], halves[3], -halves[2]], axis=0)
-    left[:, :block_rows, :] = mine.T.astype(jnp.bfloat16).reshape(blocks, block_rows, rows)
-    left[:, block_rows:, :] = swapped.T.astype(jnp.bfloat16).reshape(blocks, block_rows, rows)
+    left[:, :block_rows, :] = mine.T.astype(jnp.bfloat16).reshape(blocks, block_rows, 4 * frame_count)
+    left[:, block_rows:, :] = swapped.T.astype(jnp.bfloat16).reshape(blocks, block_rows, 4 * frame_count)
 
     def store(block):
         span = pl.ds(pl.multiple_of(block * block_rows, block_rows), block_rows)
@@ -194,14 +186,14 @@
     owners = total_feeds // ROWS_DEV
     spectra_count = TIME_BLOCKS * frame_count
     columns = 2 * channels
-    rows = 4 * frame_count
+    rows = 3 * frame_count
     lines = devices // CORES
     dft = jnp.asarray(dft_rows(fft_len, FIRST_CH, channels))
     in_vmem = pl.BlockSpec(memory_space=pltpu.VMEM)
     outgoing = pl.pallas_call(
         functools.partial(spectra_kernel, owners),
         out_shape=jax.ShapeDtypeStruct((lines, rows, feed_count), jnp.bfloat16),
-        in_specs=[pl.BlockSpec(memory_space=pl.ANY)] * 3,
+        in_specs=[pl.BlockSpec(memory_space=pltpu.HBM)] * 3,
         out_specs=in_vmem,
         scratch_shapes=[
             pltpu.VMEM(pfb_taps.shape, jnp.float32),
@@ -214,9 +206,9 @@
             pltpu.SemaphoreType.DMA((2,)),
             pltpu.SemaphoreType.DMA((frame_count * PIECES,)),
         ],
-        compiler_params=pltpu.CompilerParams(vmem_limit_bytes=56 * 2**20),
+        compiler_params=pltpu.CompilerParams(vmem_limit_bytes=44 * 2**20),
         name="spectra",
-    )(samples, pfb_taps, dft)
+    )(*[pltpu.with_memory_space_constraint(v, pltpu.HBM) for v in (samples, pfb_taps, dft)])
     same_core = [[line * CORES + core for line in range(lines)] for core in range(CORES)]
     own = lax.all_to_all(outgoing, "feed", 0, 0, axis_index_groups=same_core, tiled=True)
     other = lax.ppermute(own, "feed", [(d, d ^ 1) for d in range(devices)])
@@ -227,8 +219,8 @@
         in_specs=[in_vmem, in_vmem],
         out_specs=pl.BlockSpec(memory_space=pl.ANY),
         scratch_shapes=[
-            pltpu.VMEM((rows, total_feeds), jnp.bfloat16),
-            pltpu.VMEM((blocks, 2 * BLOCK_ROWS, rows), jnp.bfloat16),
+            pltpu.VMEM((2 * spectra_count, total_feeds), jnp.bfloat16),
+            pltpu.VMEM((blocks, 2 * BLOCK_ROWS, 2 * spectra_count), jnp.bfloat16),
             pltpu.VMEM((ROWS_DEV, 2 * total_feeds), jnp.float32),
             pltpu.SemaphoreType.DMA((blocks,)),
         ],

time: 33.6 us -> 32.4 us (0.964)
  Pallas kernels: 17.3 us -> 16.7 us
  blocking collectives: 14.6 us -> 14.2 us
    pallas_call x1, Pallas kernels: 13.5 us -> 12.9 us  [body(): pl.pallas_call(functools.partial(spectra_kernel, owners), out_shape=jax.S...]
    all_to_all x1, blocking collectives: 14.6 us -> 14.2 us  [body(): lax.all_to_all(outgoing, 'feed', 0, 0, axis_index_groups=same_core, tiled...]
where the time goes in v4:
time: 32.4 us; the launch traced here: 32.2 us
  Pallas kernels  16.7 us (52%)
  blocking collectives  14.2 us (44%)
  waiting for transfers between devices  1.3 us (4%)
    all_to_all x1, blocking collectives, body(): lax.all_to_all(outgoing, 'feed', 0, 0, axis_index_groups=same_core, tiled...  14.2 us
    pallas_call x1, Pallas kernels, body(): pl.pallas_call(functools.partial(spectra_kernel, owners), out_shape=jax.S...  12.9 us
    pallas_call x1, Pallas kernels, body(): pl.pallas_call(functools.partial(correlate_kernel, 1.0 / spectra_count, o...  3.82 us
    ppermute x1, waiting for transfers between devices, body(): other = lax.ppermute(own, 'feed', [(d, d ^ 1) for d in range(devices)])  1.3 us
  transfers between devices with their start and end apart: 1, of which 1 were waited for; matrix products, arithmetic and copies ran while one was open for 0% of the time, Pallas kernels for 0%

profile of v4, /device:TPU:0, one launch (start us, length us, event | category | flops | bytes accessed | tf_op | source)
XLA Modules:
  0.0 32.2 jit_solution(2666960445905998631)
XLA Ops:
  0.0 12.9 %spectra.1 = bf16[8,24,256]{2,1,0:T(8,128)(2,1)S(1)} custom-call(bf16[1,256,65536]{2,1,0:T(8,128)(2,1)} %x_hbm.1, f32[4,8192]{1,0:T(4,128)} %taps_hbm.1, f32[8,8192]{1,0:T(8,128)} %constant.2.clone.dft_hbm), custom_call_target="tpu_custom_call" | custom-call | tf_op jit(solution)/shard_map/spectra/pallas_call | solution.py:193
  12.9 14.2 %all_to_all.5.own_ref = bf16[8,24,256]{2,1,0:T(8,128)(2,1)S(1)} all-to-all(bf16[8,24,256]{2,1,0:T(8,128)(2,1)S(1)} %spectra.1), channel_id=1, replica_groups={{0,2,4,6,8,10,12,14},{1,3,5,7,9,11,13,15},{16,18,20,22,24,26,28,30},{17..., dimensions={0} | all-to-all | bytes 196608 | tf_op jit(solution)/shard_map/all_to_all | solution.py:213
  27.1 0.0 collective-permute-start
  27.1 1.3 %collective-permute-done.other_ref = bf16[8,24,256]{2,1,0:T(8,128)(2,1)S(1)} collective-permute-done((bf16[8,24,256]{2,1,0:T(8,128)(2,1)S(1)}, bf16[8,24,256]{2,1,0:T(8,128)(2,1)S(1)}, u32[]{:S(2)}, u32[]{:S(2)}) %collective-permute-start) | collective-permute-done | bytes 98336 | tf_op jit(solution)/shard_map/ppermute | solution.py:214
  28.4 3.8 %correlate.1 = f32[512,4096]{1,0:T(8,128)} custom-call(bf16[8,24,256]{2,1,0:T(8,128)(2,1)S(1)} %all_to_all.5.own_ref, bf16[8,24,256]{2,1,0:T(8,128)(2,1)S(1)} %collective-permute-done.other_ref), custom_call_target="tpu_custom_call" | custom-call | tf_op jit(solution)/shard_map/correlate/pallas_call | solution.py:216
Async XLA Ops:
  27.1 1.3 %collective-permute-start = (bf16[8,24,256]{2,1,0:T(8,128)(2,1)S(1)}, bf16[8,24,256]{2,1,0:T(8,128)(2,1)S(1)}, u32[]{:S(2)}, u32[]{:S(2)}) collective-permute-start(bf16[8,24,256]{2,1,0:T(8,128)(2,1)S(1)} %all_to_all.5.own_ref), channel_id=1, source_target_pairs={{0,1},{1,0},{2,3},{3,2},{4,5},{5,4},{6,7},{7,6},{8,9},{9,8},{10,11... | collective-permute-start | bytes 294920 | tf_op jit(solution)/shard_map/ppermute | solution.py:214

commit v5 on v4

--- a/solution.py
+++ b/solution.py
@@ -13,7 +13,7 @@
 TIME_BLOCKS = 2
 ROWS_DEV = 512
 CORES = 2
-PIECES = 4
+PIECES = 8
 TABLE_STEP = 1024
 BLOCK_ROWS = 64
 
@@ -94,17 +94,17 @@
         raw[...] = two_dots(frame, 0, fft_len // 2)
 
     last = frame_count - 1
+    fold(last - 1, raw[...])
+    for spot in range(last):
+        parts[:, spot, :] = window[spot]
     total = None
-    for p in range(0, PIECES, 2):
-        for k in (p, p + 1):
-            fetch(last * PIECES + k).wait()
-        if p == 0:
-            fold(last - 1, raw[...])
-        product = two_dots(last, p * piece, piece)
+    for begin, end in ((0, PIECES // 2), (PIECES // 2, 3 * PIECES // 4), (3 * PIECES // 4, PIECES)):
+        for p in range(begin, end):
+            fetch(last * PIECES + p).wait()
+        product = two_dots(last, begin * piece, (end - begin) * piece // 2)
         total = product if total is None else total + product
     fold(last, total)
-
-    for spot in range(frame_count + edge):
+    for spot in range(last, frame_count + edge):
         parts[:, spot, :] = window[spot]
 
     copies = out_ref.shape[0] // channels
@@ -129,7 +129,6 @@
     scale, owners, own_ref, other_ref, out_hbm, right, left, out_buf, sems
 ):
     lines, rows, feed_count = own_ref.shape
-    group_span = lines * CORES // TIME_BLOCKS
     frame_count = rows // 3
     total_feeds = right.shape[1]
     blocks = left.shape[0]
@@ -137,21 +136,28 @@
     my_index = lax.axis_index("feed")
     my_core = my_index % CORES
 
-    def arrived(device):
-        mine, core = device // CORES, device % CORES
-        return jnp.where(my_core == core, own_ref[mine], other_ref[mine])
-
-    for g in range(group_span):
-        span = slice(g * feed_count, (g + 1) * feed_count)
-        low, high = arrived(g), arrived(group_span + g)
-        first = low.astype(jnp.float32)
-        second = high.astype(jnp.float32)
-        extra = first[2 * frame_count :] + second[2 * frame_count :]
+    def join(group, low, high):
+        span = pl.ds(group * feed_count, feed_count)
+        if not isinstance(group, int):
+            span = pl.ds(pl.multiple_of(group * feed_count, feed_count), feed_count)
+        extra = low[2 * frame_count :].astype(jnp.float32) + high[2 * frame_count :].astype(jnp.float32)
         zero = jnp.zeros((frame_count - 4, feed_count), jnp.float32)
         extra = jnp.concatenate([extra[:4], zero, extra[4:8], zero], axis=0)
-        fixed = second[: 2 * frame_count] + extra
+        fixed = high[: 2 * frame_count].astype(jnp.float32) + extra
         right[: 2 * frame_count, span] = low[: 2 * frame_count]
         right[2 * frame_count :, span] = fixed.astype(jnp.bfloat16)
+
+    later = lines // TIME_BLOCKS
+    for line in range(later):
+        if feed_count % 128 == 0:
+            for ref, core in ((own_ref, my_core), (other_ref, CORES - 1 - my_core)):
+                join(line * CORES + core, ref[line], ref[later + line])
+        else:
+            for core in range(CORES):
+                low, high = [
+                    jnp.where(my_core == core, own_ref[k], other_ref[k]) for k in (line, later + line)
+                ]
+                join(line * CORES + core, low, high)
     row_start = my_index % owners * ROWS_DEV
     mine = right[:, pl.ds(pl.multiple_of(row_start, ROWS_DEV), ROWS_DEV)].astype(jnp.float32)
     halves = [mine[k * frame_count : (k + 1) * frame_count] for k in range(4)]

time: 32.4 us -> 32.9 us (1.015)
  Pallas kernels: 16.7 us -> 17.2 us
    pallas_call x1, Pallas kernels: 12.9 us -> 13.4 us  [body(): pl.pallas_call(functools.partial(spectra_kernel, owners), out_shape=jax.S...]
where the time goes in v5:
time: 32.9 us; the launch traced here: 32.7 us
  Pallas kernels  17.2 us (52%)
  blocking collectives  14.2 us (43%)
  waiting for transfers between devices  1.3 us (4%)
    all_to_all x1, blocking collectives, body(): lax.all_to_all(outgoing, 'feed', 0, 0, axis_index_groups=same_core, tiled...  14.2 us
    pallas_call x1, Pallas kernels, body(): pl.pallas_call(functools.partial(spectra_kernel, owners), out_shape=jax.S...  13.4 us
    pallas_call x1, Pallas kernels, body(): pl.pallas_call(functools.partial(correlate_kernel, 1.0 / spectra_count, o...  3.8 us
    ppermute x1, waiting for transfers between devices, body(): other = lax.ppermute(own, 'feed', [(d, d ^ 1) for d in range(devices)])  1.3 us
  transfers between devices with their start and end apart: 1, of which 1 were waited for; matrix products, arithmetic and copies ran while one was open for 0% of the time, Pallas kernels for 0%

profile of v5, /device:TPU:0, one launch (start us, length us, event | category | flops | bytes accessed | tf_op | source)
XLA Modules:
  0.0 32.7 jit_solution(7651256281958363320)
XLA Ops:
  0.0 13.4 %spectra.1 = bf16[8,24,256]{2,1,0:T(8,128)(2,1)S(1)} custom-call(bf16[1,256,65536]{2,1,0:T(8,128)(2,1)} %x_hbm.1, f32[4,8192]{1,0:T(4,128)} %taps_hbm.1, f32[8,8192]{1,0:T(8,128)} %constant.2.clone.dft_hbm), custom_call_target="tpu_custom_call" | custom-call | tf_op jit(solution)/shard_map/spectra/pallas_call | solution.py:199
  13.4 14.2 %all_to_all.5.own_ref = bf16[8,24,256]{2,1,0:T(8,128)(2,1)S(1)} all-to-all(bf16[8,24,256]{2,1,0:T(8,128)(2,1)S(1)} %spectra.1), channel_id=1, replica_groups={{0,2,4,6,8,10,12,14},{1,3,5,7,9,11,13,15},{16,18,20,22,24,26,28,30},{17..., dimensions={0} | all-to-all | bytes 196608 | tf_op jit(solution)/shard_map/all_to_all | solution.py:219
  27.6 0.0 collective-permute-start
  27.6 1.3 %collective-permute-done.other_ref = bf16[8,24,256]{2,1,0:T(8,128)(2,1)S(1)} collective-permute-done((bf16[8,24,256]{2,1,0:T(8,128)(2,1)S(1)}, bf16[8,24,256]{2,1,0:T(8,128)(2,1)S(1)}, u32[]{:S(2)}, u32[]{:S(2)}) %collective-permute-start) | collective-permute-done | bytes 98336 | tf_op jit(solution)/shard_map/ppermute | solution.py:220
  28.9 3.8 %correlate.1 = f32[512,4096]{1,0:T(8,128)} custom-call(bf16[8,24,256]{2,1,0:T(8,128)(2,1)S(1)} %all_to_all.5.own_ref, bf16[8,24,256]{2,1,0:T(8,128)(2,1)S(1)} %collective-permute-done.other_ref), custom_call_target="tpu_custom_call" | custom-call | tf_op jit(solution)/shard_map/correlate/pallas_call | solution.py:222
Async XLA Ops:
  27.6 1.3 %collective-permute-start = (bf16[8,24,256]{2,1,0:T(8,128)(2,1)S(1)}, bf16[8,24,256]{2,1,0:T(8,128)(2,1)S(1)}, u32[]{:S(2)}, u32[]{:S(2)}) collective-permute-start(bf16[8,24,256]{2,1,0:T(8,128)(2,1)S(1)} %all_to_all.5.own_ref), channel_id=1, source_target_pairs={{0,1},{1,0},{2,3},{3,2},{4,5},{5,4},{6,7},{7,6},{8,9},{9,8},{10,11... | collective-permute-start | bytes 294920 | tf_op jit(solution)/shard_map/ppermute | solution.py:220

commit v6 on v5

--- a/solution.py
+++ b/solution.py
@@ -13,7 +13,7 @@
 TIME_BLOCKS = 2
 ROWS_DEV = 512
 CORES = 2
-PIECES = 8
+PIECES = 4
 TABLE_STEP = 1024
 BLOCK_ROWS = 64
 
@@ -55,18 +55,16 @@
         fetch(index).start()
 
     window[...] = jnp.zeros_like(window)
-    raw[...] = jnp.zeros_like(raw)
     for copy in small:
         copy.wait()
 
-    @pl.loop(0, fft_len // TABLE_STEP)
-    def _(index):
-        span = pl.ds(pl.multiple_of(index * TABLE_STEP, TABLE_STEP), TABLE_STEP)
+    def build(start):
+        span = slice(start, start + TABLE_STEP)
         dft = dft_ref[:, span]
         scaled = jnp.concatenate([taps_ref[m : m + 1, span] * dft for m in range(tap_count)], axis=0)
-        high = scaled.astype(jnp.bfloat16).astype(jnp.float32)
-        both = jnp.concatenate([high, scaled - high], axis=0)
-        table[span, :] = both.T.astype(jnp.bfloat16)
+        high = scaled.astype(jnp.bfloat16)
+        low = (scaled - high.astype(jnp.float32)).astype(jnp.bfloat16)
+        table[span, :] = jnp.concatenate([high, low], axis=0).T
 
     def fold(frame, total):
         turned = total.T
@@ -86,25 +84,40 @@
             total = product if total is None else total + product
         return total
 
-    @pl.loop(0, frame_count - 1)
+    build(0)
+    for p in range(PIECES):
+        fetch(p).wait()
+    total = None
+    for start in range(0, fft_len, TABLE_STEP):
+        product = jnp.dot(
+            x_buf[:, start : start + TABLE_STEP],
+            table[start : start + TABLE_STEP, :],
+            preferred_element_type=jnp.float32,
+        )
+        total = product if total is None else total + product
+        if start + TABLE_STEP < fft_len:
+            build(start + TABLE_STEP)
+    raw[...] = total
+
+    @pl.loop(1, frame_count - 1)
     def _(frame):
         for p in range(PIECES):
             fetch(frame * PIECES + p).wait()
-        fold(jnp.maximum(frame - 1, 0), raw[...])
+        fold(frame - 1, raw[...])
         raw[...] = two_dots(frame, 0, fft_len // 2)
 
     last = frame_count - 1
-    fold(last - 1, raw[...])
-    for spot in range(last):
-        parts[:, spot, :] = window[spot]
     total = None
-    for begin, end in ((0, PIECES // 2), (PIECES // 2, 3 * PIECES // 4), (3 * PIECES // 4, PIECES)):
-        for p in range(begin, end):
-            fetch(last * PIECES + p).wait()
-        product = two_dots(last, begin * piece, (end - begin) * piece // 2)
+    for p in range(0, PIECES, 2):
+        for k in (p, p + 1):
+            fetch(last * PIECES + k).wait()
+        if p == 0:
+            fold(last - 1, raw[...])
+        product = two_dots(last, p * piece, piece)
         total = product if total is None else total + product
     fold(last, total)
-    for spot in range(last, frame_count + edge):
+
+    for spot in range(frame_count + edge):
         parts[:, spot, :] = window[spot]
 
     copies = out_ref.shape[0] // channels

time: 32.9 us -> 32.5 us (0.988)
  Pallas kernels: 17.2 us -> 16.8 us
    pallas_call x1, Pallas kernels: 13.4 us -> 13 us  [body(): pl.pallas_call(functools.partial(spectra_kernel, owners), out_shape=jax.S...]
where the time goes in v6:
time: 32.5 us; the launch traced here: 32.3 us
  Pallas kernels  16.8 us (52%)
  blocking collectives  14.2 us (44%)
  waiting for transfers between devices  1.3 us (4%)
    all_to_all x1, blocking collectives, body(): lax.all_to_all(outgoing, 'feed', 0, 0, axis_index_groups=same_core, tiled...  14.2 us
    pallas_call x1, Pallas kernels, body(): pl.pallas_call(functools.partial(spectra_kernel, owners), out_shape=jax.S...  13 us
    pallas_call x1, Pallas kernels, body(): pl.pallas_call(functools.partial(correlate_kernel, 1.0 / spectra_count, o...  3.8 us
    ppermute x1, waiting for transfers between devices, body(): other = lax.ppermute(own, 'feed', [(d, d ^ 1) for d in range(devices)])  1.3 us
  transfers between devices with their start and end apart: 1, of which 1 were waited for; matrix products, arithmetic and copies ran while one was open for 0% of the time, Pallas kernels for 0%

profile of v6, /device:TPU:0, one launch (start us, length us, event | category | flops | bytes accessed | tf_op | source)
XLA Modules:
  0.0 32.3 jit_solution(7518225678193293641)
XLA Ops:
  0.0 13.0 %spectra.1 = bf16[8,24,256]{2,1,0:T(8,128)(2,1)S(1)} custom-call(bf16[1,256,65536]{2,1,0:T(8,128)(2,1)} %x_hbm.1, f32[4,8192]{1,0:T(4,128)} %taps_hbm.1, f32[8,8192]{1,0:T(8,128)} %constant.2.clone.dft_hbm), custom_call_target="tpu_custom_call" | custom-call | tf_op jit(solution)/shard_map/spectra/pallas_call | solution.py:212
  13.0 14.2 %all_to_all.5.own_ref = bf16[8,24,256]{2,1,0:T(8,128)(2,1)S(1)} all-to-all(bf16[8,24,256]{2,1,0:T(8,128)(2,1)S(1)} %spectra.1), channel_id=1, replica_groups={{0,2,4,6,8,10,12,14},{1,3,5,7,9,11,13,15},{16,18,20,22,24,26,28,30},{17..., dimensions={0} | all-to-all | bytes 196608 | tf_op jit(solution)/shard_map/all_to_all | solution.py:232
  27.2 0.0 collective-permute-start
  27.2 1.3 %collective-permute-done.other_ref = bf16[8,24,256]{2,1,0:T(8,128)(2,1)S(1)} collective-permute-done((bf16[8,24,256]{2,1,0:T(8,128)(2,1)S(1)}, bf16[8,24,256]{2,1,0:T(8,128)(2,1)S(1)}, u32[]{:S(2)}, u32[]{:S(2)}) %collective-permute-start) | collective-permute-done | bytes 98336 | tf_op jit(solution)/shard_map/ppermute | solution.py:233
  28.5 3.8 %correlate.1 = f32[512,4096]{1,0:T(8,128)} custom-call(bf16[8,24,256]{2,1,0:T(8,128)(2,1)S(1)} %all_to_all.5.own_ref, bf16[8,24,256]{2,1,0:T(8,128)(2,1)S(1)} %collective-permute-done.other_ref), custom_call_target="tpu_custom_call" | custom-call | tf_op jit(solution)/shard_map/correlate/pallas_call | solution.py:235
Async XLA Ops:
  27.2 1.3 %collective-permute-start = (bf16[8,24,256]{2,1,0:T(8,128)(2,1)S(1)}, bf16[8,24,256]{2,1,0:T(8,128)(2,1)S(1)}, u32[]{:S(2)}, u32[]{:S(2)}) collective-permute-start(bf16[8,24,256]{2,1,0:T(8,128)(2,1)S(1)} %all_to_all.5.own_ref), channel_id=1, source_target_pairs={{0,1},{1,0},{2,3},{3,2},{4,5},{5,4},{6,7},{7,6},{8,9},{9,8},{10,11... | collective-permute-start | bytes 294920 | tf_op jit(solution)/shard_map/ppermute | solution.py:233

commit v7 on v5

--- a/solution.py
+++ b/solution.py
@@ -13,9 +13,9 @@
 TIME_BLOCKS = 2
 ROWS_DEV = 512
 CORES = 2
-PIECES = 8
+PIECES = 4
 TABLE_STEP = 1024
-BLOCK_ROWS = 64
+COLUMNS = 256
 
 
 def dft_rows(fft_len, first_channel, channel_count):
@@ -94,17 +94,17 @@
         raw[...] = two_dots(frame, 0, fft_len // 2)
 
     last = frame_count - 1
-    fold(last - 1, raw[...])
-    for spot in range(last):
-        parts[:, spot, :] = window[spot]
     total = None
-    for begin, end in ((0, PIECES // 2), (PIECES // 2, 3 * PIECES // 4), (3 * PIECES // 4, PIECES)):
-        for p in range(begin, end):
-            fetch(last * PIECES + p).wait()
-        product = two_dots(last, begin * piece, (end - begin) * piece // 2)
+    for p in range(0, PIECES, 2):
+        for k in (p, p + 1):
+            fetch(last * PIECES + k).wait()
+        if p == 0:
+            fold(last - 1, raw[...])
+        product = two_dots(last, p * piece, piece)
         total = product if total is None else total + product
     fold(last, total)
-    for spot in range(last, frame_count + edge):
+
+    for spot in range(frame_count + edge):
         parts[:, spot, :] = window[spot]
 
     copies = out_ref.shape[0] // channels
@@ -131,21 +131,19 @@
     lines, rows, feed_count = own_ref.shape
     frame_count = rows // 3
     total_feeds = right.shape[1]
-    blocks = left.shape[0]
-    block_rows = left.shape[1] // 2
     my_index = lax.axis_index("feed")
     my_core = my_index % CORES
 
     def join(group, low, high):
-        span = pl.ds(group * feed_count, feed_count)
+        place = pl.ds(group * feed_count, feed_count)
         if not isinstance(group, int):
-            span = pl.ds(pl.multiple_of(group * feed_count, feed_count), feed_count)
+            place = pl.ds(pl.multiple_of(group * feed_count, feed_count), feed_count)
         extra = low[2 * frame_count :].astype(jnp.float32) + high[2 * frame_count :].astype(jnp.float32)
         zero = jnp.zeros((frame_count - 4, feed_count), jnp.float32)
         extra = jnp.concatenate([extra[:4], zero, extra[4:8], zero], axis=0)
         fixed = high[: 2 * frame_count].astype(jnp.float32) + extra
-        right[: 2 * frame_count, span] = low[: 2 * frame_count]
-        right[2 * frame_count :, span] = fixed.astype(jnp.bfloat16)
+        right[: 2 * frame_count, place] = low[: 2 * frame_count]
+        right[2 * frame_count :, place] = fixed.astype(jnp.bfloat16)
 
     later = lines // TIME_BLOCKS
     for line in range(later):
@@ -162,24 +160,29 @@
     mine = right[:, pl.ds(pl.multiple_of(row_start, ROWS_DEV), ROWS_DEV)].astype(jnp.float32)
     halves = [mine[k * frame_count : (k + 1) * frame_count] for k in range(4)]
     swapped = jnp.concatenate([halves[1], -halves[0], halves[3], -halves[2]], axis=0)
-    left[:, :block_rows, :] = mine.T.astype(jnp.bfloat16).reshape(blocks, block_rows, 4 * frame_count)
-    left[:, block_rows:, :] = swapped.T.astype(jnp.bfloat16).reshape(blocks, block_rows, 4 * frame_count)
-
-    def store(block):
-        span = pl.ds(pl.multiple_of(block * block_rows, block_rows), block_rows)
-        return pltpu.make_async_copy(out_buf.at[span], out_hbm.at[span], sems.at[block])
-
-    @pl.loop(0, blocks)
+    left[:ROWS_DEV] = mine.T.astype(jnp.bfloat16)
+    left[ROWS_DEV:] = swapped.T.astype(jnp.bfloat16)
+
+    def span(block, part):
+        start = part * total_feeds + block * COLUMNS
+        return pl.ds(pl.multiple_of(start, COLUMNS), COLUMNS)
+
+    def store(block, part):
+        cut = span(block, part)
+        return pltpu.make_async_copy(out_buf.at[:, cut], out_hbm.at[:, cut], sems.at[block, part])
+
+    @pl.loop(0, total_feeds // COLUMNS)
     def _(block):
-        product = jnp.dot(left[block], right[...], preferred_element_type=jnp.float32) * scale
-        span = pl.ds(pl.multiple_of(block * block_rows, block_rows), block_rows)
-        out_buf[span, :total_feeds] = product[:block_rows]
-        out_buf[span, total_feeds:] = product[block_rows:]
-        store(block).start()
-
-    @pl.loop(0, blocks)
+        product = jnp.dot(left[...], right[:, span(block, 0)], preferred_element_type=jnp.float32)
+        product = product * scale
+        for part in range(2):
+            out_buf[:, span(block, part)] = product[part * ROWS_DEV : (part + 1) * ROWS_DEV]
+            store(block, part).start()
+
+    @pl.loop(0, total_feeds // COLUMNS)
     def _(block):
-        store(block).wait()
+        for part in range(2):
+            store(block, part).wait()
 
 
 def body(samples, pfb_taps):
@@ -218,7 +221,6 @@
     same_core = [[line * CORES + core for line in range(lines)] for core in range(CORES)]
     own = lax.all_to_all(outgoing, "feed", 0, 0, axis_index_groups=same_core, tiled=True)
     other = lax.ppermute(own, "feed", [(d, d ^ 1) for d in range(devices)])
-    blocks = ROWS_DEV // BLOCK_ROWS
     return pl.pallas_call(
         functools.partial(correlate_kernel, 1.0 / spectra_count, owners),
         out_shape=jax.ShapeDtypeStruct((ROWS_DEV, 2 * total_feeds), jnp.float32),
@@ -226,9 +228,9 @@
         out_specs=pl.BlockSpec(memory_space=pl.ANY),
         scratch_shapes=[
             pltpu.VMEM((2 * spectra_count, total_feeds), jnp.bfloat16),
-            pltpu.VMEM((blocks, 2 * BLOCK_ROWS, 2 * spectra_count), jnp.bfloat16),
+            pltpu.VMEM((2 * ROWS_DEV, 2 * spectra_count), jnp.bfloat16),
             pltpu.VMEM((ROWS_DEV, 2 * total_feeds), jnp.float32),
-            pltpu.SemaphoreType.DMA((blocks,)),
+            pltpu.SemaphoreType.DMA((total_feeds // COLUMNS, 2)),
         ],
         compiler_params=pltpu.CompilerParams(vmem_limit_bytes=32 * 2**20),
         name="correlate",

time: 32.9 us -> 32.4 us (0.985)
  Pallas kernels: 17.2 us -> 16.7 us
    pallas_call x1, Pallas kernels: 13.4 us -> 12.9 us  [body(): pl.pallas_call(functools.partial(spectra_kernel, owners), out_shape=jax.S...]
where the time goes in v7:
time: 32.4 us; the launch traced here: 32.2 us
  Pallas kernels  16.7 us (52%)
  blocking collectives  14.2 us (44%)
  waiting for transfers between devices  1.3 us (4%)
    all_to_all x1, blocking collectives, body(): lax.all_to_all(outgoing, 'feed', 0, 0, axis_index_groups=same_core, tiled...  14.2 us
    pallas_call x1, Pallas kernels, body(): pl.pallas_call(functools.partial(spectra_kernel, owners), out_shape=jax.S...  12.9 us
    pallas_call x1, Pallas kernels, body(): pl.pallas_call(functools.partial(correlate_kernel, 1.0 / spectra_count, o...  3.86 us
    ppermute x1, waiting for transfers between devices, body(): other = lax.ppermute(own, 'feed', [(d, d ^ 1) for d in range(devices)])  1.3 us
  transfers between devices with their start and end apart: 1, of which 1 were waited for; matrix products, arithmetic and copies ran while one was open for 0% of the time, Pallas kernels for 0%

profile of v7, /device:TPU:0, one launch (start us, length us, event | category | flops | bytes accessed | tf_op | source)
XLA Modules:
  0.0 32.2 jit_solution(13713553185181120426)
XLA Ops:
  0.0 12.9 %spectra.1 = bf16[8,24,256]{2,1,0:T(8,128)(2,1)S(1)} custom-call(bf16[1,256,65536]{2,1,0:T(8,128)(2,1)} %x_hbm.1, f32[4,8192]{1,0:T(4,128)} %taps_hbm.1, f32[8,8192]{1,0:T(8,128)} %constant.2.clone.dft_hbm), custom_call_target="tpu_custom_call" | custom-call | tf_op jit(solution)/shard_map/spectra/pallas_call | solution.py:202
  12.9 14.2 %all_to_all.5.own_ref = bf16[8,24,256]{2,1,0:T(8,128)(2,1)S(1)} all-to-all(bf16[8,24,256]{2,1,0:T(8,128)(2,1)S(1)} %spectra.1), channel_id=1, replica_groups={{0,2,4,6,8,10,12,14},{1,3,5,7,9,11,13,15},{16,18,20,22,24,26,28,30},{17..., dimensions={0} | all-to-all | bytes 196608 | tf_op jit(solution)/shard_map/all_to_all | solution.py:222
  27.1 0.0 collective-permute-start
  27.1 1.3 %collective-permute-done.other_ref = bf16[8,24,256]{2,1,0:T(8,128)(2,1)S(1)} collective-permute-done((bf16[8,24,256]{2,1,0:T(8,128)(2,1)S(1)}, bf16[8,24,256]{2,1,0:T(8,128)(2,1)S(1)}, u32[]{:S(2)}, u32[]{:S(2)}) %collective-permute-start) | collective-permute-done | bytes 98336 | tf_op jit(solution)/shard_map/ppermute | solution.py:223
  28.4 3.9 %correlate.1 = f32[512,4096]{1,0:T(8,128)} custom-call(bf16[8,24,256]{2,1,0:T(8,128)(2,1)S(1)} %all_to_all.5.own_ref, bf16[8,24,256]{2,1,0:T(8,128)(2,1)S(1)} %collective-permute-done.other_ref), custom_call_target="tpu_custom_call" | custom-call | tf_op jit(solution)/shard_map/correlate/pallas_call | solution.py:224
Async XLA Ops:
  27.1 1.3 %collective-permute-start = (bf16[8,24,256]{2,1,0:T(8,128)(2,1)S(1)}, bf16[8,24,256]{2,1,0:T(8,128)(2,1)S(1)}, u32[]{:S(2)}, u32[]{:S(2)}) collective-permute-start(bf16[8,24,256]{2,1,0:T(8,128)(2,1)S(1)} %all_to_all.5.own_ref), channel_id=1, source_target_pairs={{0,1},{1,0},{2,3},{3,2},{4,5},{5,4},{6,7},{7,6},{8,9},{9,8},{10,11... | collective-permute-start | bytes 294920 | tf_op jit(solution)/shard_map/ppermute | solution.py:223

commit v8 on v7

--- a/solution.py
+++ b/solution.py
@@ -183,6 +183,134 @@
     def _(block):
         for part in range(2):
             store(block, part).wait()
+
+
+def join_blocks(low, high):
+    frame_count = low.shape[0] // 3
+    feed_count = low.shape[1]
+    extra = low[2 * frame_count :].astype(jnp.float32) + high[2 * frame_count :].astype(jnp.float32)
+    zero = jnp.zeros((frame_count - 4, feed_count), jnp.float32)
+    extra = jnp.concatenate([extra[:4], zero, extra[4:8], zero], axis=0)
+    fixed = high[: 2 * frame_count].astype(jnp.float32) + extra
+    return jnp.concatenate([low[: 2 * frame_count], fixed.astype(jnp.bfloat16)], axis=0)
+
+
+def left_rows(block):
+    mine = block.astype(jnp.float32)
+    size = mine.shape[0] // 4
+    parts = [mine[k * size : (k + 1) * size] for k in range(4)]
+    swapped = jnp.concatenate([parts[1], -parts[0], parts[3], -parts[2]], axis=0)
+    return jnp.concatenate([mine.T, swapped.T], axis=0).astype(jnp.bfloat16)
+
+
+def store_block(out_buf, out_hbm, sem, row_group, column_group, part):
+    size = out_hbm.shape[0] // CORES
+    row = pl.multiple_of(row_group * size, size)
+    column = pl.multiple_of(part * (out_hbm.shape[1] // 2) + column_group * size, size)
+    place = (pl.ds(row, size), pl.ds(column, size))
+    return place, pltpu.make_async_copy(out_buf.at[place], out_hbm.at[place], sem)
+
+
+def near_kernel(scale, owners, own_ref, out_hbm, right, out_buf, sems):
+    lines, _, size = own_ref.shape
+    later = lines // TIME_BLOCKS
+    my_index = lax.axis_index("feed")
+    my_core = my_index % CORES
+
+    for line in range(later):
+        right[line] = join_blocks(own_ref[line], own_ref[later + line])
+    left = left_rows(right[my_index % owners])
+    copies = []
+    for line in range(later):
+        product = jnp.dot(left, right[line], preferred_element_type=jnp.float32) * scale
+        for part in range(2):
+            place, copy = store_block(
+                out_buf, out_hbm, sems.at[line, part], my_core, line * CORES + my_core, part
+            )
+            out_buf[place] = product[part * size : (part + 1) * size]
+            copy.start()
+            copies.append(copy)
+    for copy in copies:
+        copy.wait()
+
+
+def far_kernel(scale, owners, own_ref, other_ref, _, out_hbm, near, far, left, out_buf, sems):
+    lines, _, size = own_ref.shape
+    later = lines // TIME_BLOCKS
+    my_index = lax.axis_index("feed")
+    my_core = my_index % CORES
+    other_core = CORES - 1 - my_core
+    place_in_plane = my_index % owners
+
+    for line in range(later):
+        near[line] = join_blocks(own_ref[line], own_ref[later + line])
+        far[line] = join_blocks(other_ref[line], other_ref[later + line])
+    left[0] = left_rows(near[place_in_plane])
+    left[1] = left_rows(far[place_in_plane])
+
+    def block(line, turn):
+        row_group = my_core if turn == 0 else other_core
+        column_group = line * CORES + (my_core if turn == 2 else other_core)
+        for part in range(2):
+            yield store_block(out_buf, out_hbm, sems.at[line, turn, part], row_group, column_group, part)
+
+    @pl.loop(0, later)
+    def _(line):
+        for turn in range(3):
+            source = near if turn == 2 else far
+            product = jnp.dot(left[min(turn, 1)], source[line], preferred_element_type=jnp.float32)
+            product = product * scale
+            for part, (place, copy) in enumerate(block(line, turn)):
+                out_buf[place] = product[part * size : (part + 1) * size]
+                copy.start()
+
+    @pl.loop(0, later)
+    def _(line):
+        for turn in range(3):
+            for _, copy in block(line, turn):
+                copy.wait()
+
+
+def correlate_in_two(own, swap, owners, total_feeds, scale):
+    lines, rows, size = own.shape
+    depth = rows // 3 * 4
+    later = lines // TIME_BLOCKS
+    in_vmem = pl.BlockSpec(memory_space=pltpu.VMEM)
+    anywhere = pl.BlockSpec(memory_space=pl.ANY)
+    shape = jax.ShapeDtypeStruct((ROWS_DEV, 2 * total_feeds), jnp.float32)
+    other = swap(own)
+    started = pl.pallas_call(
+        functools.partial(near_kernel, scale, owners),
+        out_shape=shape,
+        in_specs=[in_vmem],
+        out_specs=anywhere,
+        scratch_shapes=[
+            pltpu.VMEM((later, depth, size), jnp.bfloat16),
+            pltpu.VMEM(shape.shape, jnp.float32),
+            pltpu.SemaphoreType.DMA((later, 2)),
+        ],
+        cost_estimate=pl.CostEstimate(
+            flops=depth * shape.size // 2, bytes_accessed=shape.size, transcendentals=0
+        ),
+        compiler_params=pltpu.CompilerParams(vmem_limit_bytes=32 * 2**20),
+        name="near",
+    )(own)
+    return pl.pallas_call(
+        functools.partial(far_kernel, scale, owners),
+        out_shape=shape,
+        in_specs=[in_vmem, in_vmem, anywhere],
+        out_specs=anywhere,
+        input_output_aliases={2: 0},
+        scratch_shapes=[
+            pltpu.VMEM((later, depth, size), jnp.bfloat16),
+            pltpu.VMEM((later, depth, size), jnp.bfloat16),
+            pltpu.VMEM((2, 2 * size, depth), jnp.bfloat16),
+            pltpu.VMEM(shape.shape, jnp.float32),
+            pltpu.SemaphoreType.DMA((later, 3, 2)),
+        ],
+        compiler_params=pltpu.CompilerParams(vmem_limit_bytes=32 * 2**20),
+        name="far",
+    )(own, other, started)
 
 
 def body(samples, pfb_taps):
@@ -220,7 +348,13 @@
     )(*[pltpu.with_memory_space_constraint(v, pltpu.HBM) for v in (samples, pfb_taps, dft)])
     same_core = [[line * CORES + core for line in range(lines)] for core in range(CORES)]
     own = lax.all_to_all(outgoing, "feed", 0, 0, axis_index_groups=same_core, tiled=True)
-    other = lax.ppermute(own, "feed", [(d, d ^ 1) for d in range(devices)])
+
+    def swap(value):
+        return lax.ppermute(value, "feed", [(d, d ^ 1) for d in range(devices)])
+
+    if feed_count * CORES == ROWS_DEV and feed_count % 128 == 0:
+        return correlate_in_two(own, swap, owners, total_feeds, 1.0 / spectra_count)
+    other = swap(own)
     return pl.pallas_call(
         functools.partial(correlate_kernel, 1.0 / spectra_count, owners),
         out_shape=jax.ShapeDtypeStruct((ROWS_DEV, 2 * total_feeds), jnp.float32),

time: 32.4 us -> 32.2 us (level)
  waiting for transfers between devices: 1.3 us -> 0.01 us
  Pallas kernels: 16.7 us -> 17.7 us
    ppermute x1, waiting for transfers between devices: 1.3 us -> 0.01 us  [swap(): return lax.ppermute(value, 'feed', [(d, d ^ 1) for d in range(devices)])]
    pallas_call x1 -> x2, Pallas kernels: 3.86 us -> 4.87 us  [the longest x1 3.2 us: correlate_in_two(): pl.pallas_call(functools.partial(far_kernel, scale, owners), out_shape=sh...]
  transfers between devices with their start and end apart: 1 -> 1, of which waited for: 1 -> 0; matrix products, arithmetic and copies ran while one was open for 0% -> 0% of each run, Pallas kernels for 0% -> 5%
where the time goes in v8:
time: 32.2 us; the launch traced here: 32 us
  Pallas kernels  17.7 us (55%)
  blocking collectives  14.2 us (44%)
    all_to_all x1, blocking collectives, body(): lax.all_to_all(outgoing, 'feed', 0, 0, axis_index_groups=same_core, tiled...  14.2 us
    pallas_call x1, Pallas kernels, body(): pl.pallas_call(functools.partial(spectra_kernel, owners), out_shape=jax.S...  12.9 us
    pallas_call x1, Pallas kernels, correlate_in_two(): pl.pallas_call(functools.partial(far_kernel, scale, owners), out_shape=sh...  3.2 us
    pallas_call x1, Pallas kernels, correlate_in_two(): pl.pallas_call(functools.partial(near_kernel, scale, owners), out_shape=s...  1.67 us
  transfers between devices with their start and end apart: 1, of which 0 were waited for; matrix products, arithmetic and copies ran while one was open for 0% of the time, Pallas kernels for 5%

profile of v8, /device:TPU:0, one launch (start us, length us, event | category | flops | bytes accessed | tf_op | source)
XLA Modules:
  0.0 32.0 jit_solution(8747529025593808049)
XLA Ops:
  0.0 12.9 %spectra.1 = bf16[8,24,256]{2,1,0:T(8,128)(2,1)S(1)} custom-call(bf16[1,256,65536]{2,1,0:T(8,128)(2,1)} %x_hbm.1, f32[4,8192]{1,0:T(4,128)} %taps_hbm.1, f32[8,8192]{1,0:T(8,128)} %constant.2.clone.dft_hbm), custom_call_target="tpu_custom_call" | custom-call | tf_op jit(solution)/shard_map/spectra/pallas_call | solution.py:330
  12.9 14.2 %all_to_all.5.own_ref = bf16[8,24,256]{2,1,0:T(8,128)(2,1)S(1)} all-to-all(bf16[8,24,256]{2,1,0:T(8,128)(2,1)S(1)} %spectra.1), channel_id=1, replica_groups={{0,2,4,6,8,10,12,14},{1,3,5,7,9,11,13,15},{16,18,20,22,24,26,28,30},{17..., dimensions={0} | all-to-all | bytes 196608 | tf_op jit(solution)/shard_map/all_to_all | solution.py:350
  27.1 0.0 collective-permute-start
  27.1 1.7 %near.1._ = f32[512,4096]{1,0:T(8,128)} custom-call(bf16[8,24,256]{2,1,0:T(8,128)(2,1)S(1)} %all_to_all.5.own_ref), custom_call_target="tpu_custom_call" | custom-call | flops 33554432 | bytes 2097152 | tf_op jit(solution)/shard_map/near/pallas_call | solution.py:282
  28.7 0.0 collective-permute-done.other_ref
  28.8 3.2 %far.1 = f32[512,4096]{1,0:T(8,128)} custom-call(bf16[8,24,256]{2,1,0:T(8,128)(2,1)S(1)} %all_to_all.5.own_ref, bf16[8,24,256]{2,1,0:T(8,128)(2,1)S(1)} %collective-permute-done.other_ref, f32[512,4096]{1,0:T(8,128)} %near.1._), custom_call_target="tpu_custom_call", output_to_operand_aliasing={{}: (2, {})} | custom-call | tf_op jit(solution)/shard_map/far/pallas_call | solution.py:298
Async XLA Ops:
  27.1 1.7 %collective-permute-start = (bf16[8,24,256]{2,1,0:T(8,128)(2,1)S(1)}, bf16[8,24,256]{2,1,0:T(8,128)(2,1)S(1)}, u32[]{:S(2)}, u32[]{:S(2)}) collective-permute-start(bf16[8,24,256]{2,1,0:T(8,128)(2,1)S(1)} %all_to_all.5.own_ref), channel_id=1, source_target_pairs={{0,1},{1,0},{2,3},{3,2},{4,5},{5,4},{6,7},{7,6},{8,9},{9,8},{10,11... | collective-permute-start | bytes 294920 | tf_op jit(solution)/shard_map/ppermute | solution.py:353

commit v9 on v8

--- a/solution.py
+++ b/solution.py
@@ -95,12 +95,12 @@
 
     last = frame_count - 1
     total = None
-    for p in range(0, PIECES, 2):
-        for k in (p, p + 1):
-            fetch(last * PIECES + k).wait()
-        if p == 0:
+    for begin, end in ((0, PIECES // 2), *((p, p + 1) for p in range(PIECES // 2, PIECES))):
+        for p in range(begin, end):
+            fetch(last * PIECES + p).wait()
+        if begin == 0:
             fold(last - 1, raw[...])
-        product = two_dots(last, p * piece, piece)
+        product = two_dots(last, begin * piece, (end - begin) * piece // 2)
         total = product if total is None else total + product
     fold(last, total)
 
@@ -211,7 +211,7 @@
     return place, pltpu.make_async_copy(out_buf.at[place], out_hbm.at[place], sem)
 
 
-def near_kernel(scale, owners, own_ref, out_hbm, right, out_buf, sems):
+def near_kernel(scale, owners, own_ref, out_hbm, right, left, out_buf, sems):
     lines, _, size = own_ref.shape
     later = lines // TIME_BLOCKS
     my_index = lax.axis_index("feed")
@@ -219,10 +219,10 @@
 
     for line in range(later):
         right[line] = join_blocks(own_ref[line], own_ref[later + line])
-    left = left_rows(right[my_index % owners])
+    left[...] = left_rows(right[my_index % owners])
     copies = []
     for line in range(later):
-        product = jnp.dot(left, right[line], preferred_element_type=jnp.float32) * scale
+        product = jnp.dot(left[...], right[line], preferred_element_type=jnp.float32) * scale
         for part in range(2):
             place, copy = store_block(
                 out_buf, out_hbm, sems.at[line, part], my_core, line * CORES + my_core, part
@@ -234,19 +234,18 @@
         copy.wait()
 
 
-def far_kernel(scale, owners, own_ref, other_ref, _, out_hbm, near, far, left, out_buf, sems):
-    lines, _, size = own_ref.shape
+def far_kernel(
+    scale, owners, other_ref, near, near_left, _, out_hbm, far, far_left, out_buf, sems
+):
+    lines, _, size = other_ref.shape
     later = lines // TIME_BLOCKS
     my_index = lax.axis_index("feed")
     my_core = my_index % CORES
     other_core = CORES - 1 - my_core
-    place_in_plane = my_index % owners
 
     for line in range(later):
-        near[line] = join_blocks(own_ref[line], own_ref[later + line])
         far[line] = join_blocks(other_ref[line], other_ref[later + line])
-    left[0] = left_rows(near[place_in_plane])
-    left[1] = left_rows(far[place_in_plane])
+    far_left[...] = left_rows(far[my_index % owners])
 
     def block(line, turn):
         row_group = my_core if turn == 0 else other_core
@@ -258,7 +257,8 @@
     def _(line):
         for turn in range(3):
             source = near if turn == 2 else far
-            product = jnp.dot(left[min(turn, 1)], source[line], preferred_element_type=jnp.float32)
+            left = near_left if turn == 0 else far_left
+            product = jnp.dot(left[...], source[line], preferred_element_type=jnp.float32)
             product = product * scale
             for part, (place, copy) in enumerate(block(line, turn)):
                 out_buf[place] = product[part * size : (part + 1) * size]
@@ -279,13 +279,14 @@
     anywhere = pl.BlockSpec(memory_space=pl.ANY)
     shape = jax.ShapeDtypeStruct((ROWS_DEV, 2 * total_feeds), jnp.float32)
     other = swap(own)
-    started = pl.pallas_call(
+    joined = jax.ShapeDtypeStruct((later, depth, size), jnp.bfloat16)
+    left = jax.ShapeDtypeStruct((2 * size, depth), jnp.bfloat16)
+    started, near, near_left = pl.pallas_call(
         functools.partial(near_kernel, scale, owners),
-        out_shape=shape,
+        out_shape=[shape, joined, left],
         in_specs=[in_vmem],
-        out_specs=anywhere,
+        out_specs=[anywhere, in_vmem, in_vmem],
         scratch_shapes=[
-            pltpu.VMEM((later, depth, size), jnp.bfloat16),
             pltpu.VMEM(shape.shape, jnp.float32),
             pltpu.SemaphoreType.DMA((later, 2)),
         ],
@@ -298,19 +299,18 @@
     return pl.pallas_call(
         functools.partial(far_kernel, scale, owners),
         out_shape=shape,
-        in_specs=[in_vmem, in_vmem, anywhere],
+        in_specs=[in_vmem, in_vmem, in_vmem, anywhere],
         out_specs=anywhere,
-        input_output_aliases={2: 0},
+        input_output_aliases={3: 0},
         scratch_shapes=[
-            pltpu.VMEM((later, depth, size), jnp.bfloat16),
-            pltpu.VMEM((later, depth, size), jnp.bfloat16),
-            pltpu.VMEM((2, 2 * size, depth), jnp.bfloat16),
+            pltpu.VMEM(joined.shape, jnp.bfloat16),
+            pltpu.VMEM(left.shape, jnp.bfloat16),
             pltpu.VMEM(shape.shape, jnp.float32),
             pltpu.SemaphoreType.DMA((later, 3, 2)),
         ],
         compiler_params=pltpu.CompilerParams(vmem_limit_bytes=32 * 2**20),
         name="far",
-    )(own, other, started)
+    )(other, near, near_left, started)
 
 
 def body(samples, pfb_taps):

time: 32.2 us -> 32.3 us (level)
  no operation moved by 1% of the time
where the time goes in v9:
time: 32.3 us; the launch traced here: 32.1 us
  Pallas kernels  17.9 us (55%)
  blocking collectives  14.2 us (44%)
    all_to_all x1, blocking collectives, body(): lax.all_to_all(outgoing, 'feed', 0, 0, axis_index_groups=same_core, tiled...  14.2 us
    pallas_call x1, Pallas kernels, body(): pl.pallas_call(functools.partial(spectra_kernel, owners), out_shape=jax.S...  13 us
    pallas_call x1, Pallas kernels, correlate_in_two(): pl.pallas_call(functools.partial(far_kernel, scale, owners), out_shape=sh...  3.17 us
    pallas_call x1, Pallas kernels, correlate_in_two(): pl.pallas_call(functools.partial(near_kernel, scale, owners), out_shape=[...  1.68 us
  transfers between devices with their start and end apart: 1, of which 0 were waited for; matrix products, arithmetic and copies ran while one was open for 0% of the time, Pallas kernels for 5%

profile of v9, /device:TPU:0, one launch (start us, length us, event | category | flops | bytes accessed | tf_op | source)
XLA Modules:
  0.0 32.1 jit_solution(1213164493020549657)
XLA Ops:
  0.0 13.0 %spectra.1 = bf16[8,24,256]{2,1,0:T(8,128)(2,1)S(1)} custom-call(bf16[1,256,65536]{2,1,0:T(8,128)(2,1)} %x_hbm.1, f32[4,8192]{1,0:T(4,128)} %taps_hbm.1, f32[8,8192]{1,0:T(8,128)} %constant.2.clone.dft_hbm), custom_call_target="tpu_custom_call" | custom-call | tf_op jit(solution)/shard_map/spectra/pallas_call | solution.py:330
  13.0 14.2 %all_to_all.5.own_ref = bf16[8,24,256]{2,1,0:T(8,128)(2,1)S(1)} all-to-all(bf16[8,24,256]{2,1,0:T(8,128)(2,1)S(1)} %spectra.1), channel_id=1, replica_groups={{0,2,4,6,8,10,12,14},{1,3,5,7,9,11,13,15},{16,18,20,22,24,26,28,30},{17..., dimensions={0} | all-to-all | bytes 196608 | tf_op jit(solution)/shard_map/all_to_all | solution.py:350
  27.2 0.0 collective-permute-start
  27.2 1.7 %near.1 = (f32[512,4096]{1,0:T(8,128)}, bf16[4,32,256]{2,1,0:T(8,128)(2,1)S(1)}, bf16[512,32]{1,0:T(8,128)(2,1)S(1)}) custom-call(bf16[8,24,256]{2,1,0:T(8,128)(2,1)S(1)} %all_to_all.5.own_ref), custom_call_target="tpu_custom_call" | custom-call | flops 33554432 | bytes 2097152 | tf_op jit(solution)/shard_map/near/pallas_call | solution.py:284
  28.9 0.0 collective-permute-done.other_ref
  28.9 3.2 %far.1 = f32[512,4096]{1,0:T(8,128)} custom-call(bf16[8,24,256]{2,1,0:T(8,128)(2,1)S(1)} %collective-permute-done.other_ref, bf16[4,32,256]{2,1,0:T(8,128)(2,1)S(1)} %get-tuple-element.8.near, bf16[512,32]{1,0:T(8,128)(2,1)S(1)} %get-tuple-element.9.near_left, f32[512,4096]{1,0:T(8,128)} %get-tuple-element.10._), custom_call_target="tpu_custom_call", output_to_operand_aliasing={{}: (3, {})} | custom-call | tf_op jit(solution)/shard_map/far/pallas_call | solution.py:299
Async XLA Ops:
  27.2 1.7 %collective-permute-start = (bf16[8,24,256]{2,1,0:T(8,128)(2,1)S(1)}, bf16[8,24,256]{2,1,0:T(8,128)(2,1)S(1)}, u32[]{:S(2)}, u32[]{:S(2)}) collective-permute-start(bf16[8,24,256]{2,1,0:T(8,128)(2,1)S(1)} %all_to_all.5.own_ref), channel_id=1, source_target_pairs={{0,1},{1,0},{2,3},{3,2},{4,5},{5,4},{6,7},{7,6},{8,9},{9,8},{10,11... | collective-permute-start | bytes 294920 | tf_op jit(solution)/shard_map/ppermute | solution.py:353

commit v10 on v8

--- a/solution.py
+++ b/solution.py
@@ -13,7 +13,7 @@
 TIME_BLOCKS = 2
 ROWS_DEV = 512
 CORES = 2
-PIECES = 4
+PIECES = 2
 TABLE_STEP = 1024
 COLUMNS = 256
 
@@ -95,12 +95,11 @@
 
     last = frame_count - 1
     total = None
-    for p in range(0, PIECES, 2):
-        for k in (p, p + 1):
-            fetch(last * PIECES + k).wait()
+    for p in range(PIECES):
+        fetch(last * PIECES + p).wait()
         if p == 0:
             fold(last - 1, raw[...])
-        product = two_dots(last, p * piece, piece)
+        product = two_dots(last, p * piece, piece // 2)
         total = product if total is None else total + product
     fold(last, total)
 

time: 32.2 us -> 32.1 us (level)
  no operation moved by 1% of the time
where the time goes in v10:
time: 32.1 us; the launch traced here: 31.8 us
  Pallas kernels  17.6 us (55%)
  blocking collectives  14.2 us (44%)
    all_to_all x1, blocking collectives, body(): lax.all_to_all(outgoing, 'feed', 0, 0, axis_index_groups=same_core, tiled...  14.2 us
    pallas_call x1, Pallas kernels, body(): pl.pallas_call(functools.partial(spectra_kernel, owners), out_shape=jax.S...  12.7 us
    pallas_call x1, Pallas kernels, correlate_in_two(): pl.pallas_call(functools.partial(far_kernel, scale, owners), out_shape=sh...  3.2 us
    pallas_call x1, Pallas kernels, correlate_in_two(): pl.pallas_call(functools.partial(near_kernel, scale, owners), out_shape=s...  1.67 us
  transfers between devices with their start and end apart: 1, of which 0 were waited for; matrix products, arithmetic and copies ran while one was open for 0% of the time, Pallas kernels for 5%

profile of v10, /device:TPU:0, one launch (start us, length us, event | category | flops | bytes accessed | tf_op | source)
XLA Modules:
  0.0 31.8 jit_solution(10856794183877442141)
XLA Ops:
  0.0 12.7 %spectra.1 = bf16[8,24,256]{2,1,0:T(8,128)(2,1)S(1)} custom-call(bf16[1,256,65536]{2,1,0:T(8,128)(2,1)} %x_hbm.1, f32[4,8192]{1,0:T(4,128)} %taps_hbm.1, f32[8,8192]{1,0:T(8,128)} %constant.2.clone.dft_hbm), custom_call_target="tpu_custom_call" | custom-call | tf_op jit(solution)/shard_map/spectra/pallas_call | solution.py:329
  12.7 14.2 %all_to_all.5.own_ref = bf16[8,24,256]{2,1,0:T(8,128)(2,1)S(1)} all-to-all(bf16[8,24,256]{2,1,0:T(8,128)(2,1)S(1)} %spectra.1), channel_id=1, replica_groups={{0,2,4,6,8,10,12,14},{1,3,5,7,9,11,13,15},{16,18,20,22,24,26,28,30},{17..., dimensions={0} | all-to-all | bytes 196608 | tf_op jit(solution)/shard_map/all_to_all | solution.py:349
  26.9 0.0 collective-permute-start
  26.9 1.7 %near.1._ = f32[512,4096]{1,0:T(8,128)} custom-call(bf16[8,24,256]{2,1,0:T(8,128)(2,1)S(1)} %all_to_all.5.own_ref), custom_call_target="tpu_custom_call" | custom-call | flops 33554432 | bytes 2097152 | tf_op jit(solution)/shard_map/near/pallas_call | solution.py:281
  28.6 0.0 collective-permute-done.other_ref
  28.6 3.2 %far.1 = f32[512,4096]{1,0:T(8,128)} custom-call(bf16[8,24,256]{2,1,0:T(8,128)(2,1)S(1)} %all_to_all.5.own_ref, bf16[8,24,256]{2,1,0:T(8,128)(2,1)S(1)} %collective-permute-done.other_ref, f32[512,4096]{1,0:T(8,128)} %near.1._), custom_call_target="tpu_custom_call", output_to_operand_aliasing={{}: (2, {})} | custom-call | tf_op jit(solution)/shard_map/far/pallas_call | solution.py:297
Async XLA Ops:
  26.9 1.7 %collective-permute-start = (bf16[8,24,256]{2,1,0:T(8,128)(2,1)S(1)}, bf16[8,24,256]{2,1,0:T(8,128)(2,1)S(1)}, u32[]{:S(2)}, u32[]{:S(2)}) collective-permute-start(bf16[8,24,256]{2,1,0:T(8,128)(2,1)S(1)} %all_to_all.5.own_ref), channel_id=1, source_target_pairs={{0,1},{1,0},{2,3},{3,2},{4,5},{5,4},{6,7},{7,6},{8,9},{9,8},{10,11... | collective-permute-start | bytes 294920 | tf_op jit(solution)/shard_map/ppermute | solution.py:352

commit v11 on v10

--- a/solution.py
+++ b/solution.py
@@ -210,18 +210,18 @@
     return place, pltpu.make_async_copy(out_buf.at[place], out_hbm.at[place], sem)
 
 
-def near_kernel(scale, owners, own_ref, out_hbm, right, out_buf, sems):
+def near_kernel(scale, owners, own_ref, out_hbm, out_buf, sems):
     lines, _, size = own_ref.shape
     later = lines // TIME_BLOCKS
     my_index = lax.axis_index("feed")
     my_core = my_index % CORES
 
-    for line in range(later):
-        right[line] = join_blocks(own_ref[line], own_ref[later + line])
-    left = left_rows(right[my_index % owners])
+    my_line = my_index % owners
+    left = left_rows(join_blocks(own_ref[my_line], own_ref[later + my_line]))
     copies = []
     for line in range(later):
-        product = jnp.dot(left, right[line], preferred_element_type=jnp.float32) * scale
+        right = join_blocks(own_ref[line], own_ref[later + line])
+        product = jnp.dot(left, right, preferred_element_type=jnp.float32) * scale
         for part in range(2):
             place, copy = store_block(
                 out_buf, out_hbm, sems.at[line, part], my_core, line * CORES + my_core, part
@@ -233,7 +233,7 @@
         copy.wait()
 
 
-def far_kernel(scale, owners, own_ref, other_ref, _, out_hbm, near, far, left, out_buf, sems):
+def far_kernel(scale, owners, own_ref, other_ref, _, out_hbm, left, out_buf, sems):
     lines, _, size = own_ref.shape
     later = lines // TIME_BLOCKS
     my_index = lax.axis_index("feed")
@@ -241,11 +241,8 @@
     other_core = CORES - 1 - my_core
     place_in_plane = my_index % owners
 
-    for line in range(later):
-        near[line] = join_blocks(own_ref[line], own_ref[later + line])
-        far[line] = join_blocks(other_ref[line], other_ref[later + line])
-    left[0] = left_rows(near[place_in_plane])
-    left[1] = left_rows(far[place_in_plane])
+    for k, ref in enumerate((own_ref, other_ref)):
+        left[k] = left_rows(join_blocks(ref[place_in_plane], ref[later + place_in_plane]))
 
     def block(line, turn):
         row_group = my_core if turn == 0 else other_core
@@ -255,9 +252,11 @@
 
     @pl.loop(0, later)
     def _(line):
+        far = join_blocks(other_ref[line], other_ref[later + line])
+        near = join_blocks(own_ref[line], own_ref[later + line])
         for turn in range(3):
             source = near if turn == 2 else far
-            product = jnp.dot(left[min(turn, 1)], source[line], preferred_element_type=jnp.float32)
+            product = jnp.dot(left[min(turn, 1)], source, preferred_element_type=jnp.float32)
             product = product * scale
             for part, (place, copy) in enumerate(block(line, turn)):
                 out_buf[place] = product[part * size : (part + 1) * size]
@@ -284,7 +283,6 @@
         in_specs=[in_vmem],
         out_specs=anywhere,
         scratch_shapes=[
-            pltpu.VMEM((later, depth, size), jnp.bfloat16),
             pltpu.VMEM(shape.shape, jnp.float32),
             pltpu.SemaphoreType.DMA((later, 2)),
         ],
@@ -301,8 +299,6 @@
         out_specs=anywhere,
         input_output_aliases={2: 0},
         scratch_shapes=[
-            pltpu.VMEM((later, depth, size), jnp.bfloat16),
-            pltpu.VMEM((later, depth, size), jnp.bfloat16),
             pltpu.VMEM((2, 2 * size, depth), jnp.bfloat16),
             pltpu.VMEM(shape.shape, jnp.float32),
             pltpu.SemaphoreType.DMA((later, 3, 2)),

time: 32.1 us -> 32.1 us (level)
  no operation moved by 1% of the time
where the time goes in v11:
time: 32.1 us; the launch traced here: 31.8 us
  Pallas kernels  17.6 us (55%)
  blocking collectives  14.2 us (44%)
    all_to_all x1, blocking collectives, body(): lax.all_to_all(outgoing, 'feed', 0, 0, axis_index_groups=same_core, tiled...  14.2 us
    pallas_call x1, Pallas kernels, body(): pl.pallas_call(functools.partial(spectra_kernel, owners), out_shape=jax.S...  12.7 us
    pallas_call x1, Pallas kernels, correlate_in_two(): pl.pallas_call(functools.partial(far_kernel, scale, owners), out_shape=sh...  3.2 us
    pallas_call x1, Pallas kernels, correlate_in_two(): pl.pallas_call(functools.partial(near_kernel, scale, owners), out_shape=s...  1.66 us
  transfers between devices with their start and end apart: 1, of which 0 were waited for; matrix products, arithmetic and copies ran while one was open for 0% of the time, Pallas kernels for 5%

profile of v11, /device:TPU:0, one launch (start us, length us, event | category | flops | bytes accessed | tf_op | source)
XLA Modules:
  0.0 31.8 jit_solution(9600798626007101349)
XLA Ops:
  0.0 12.7 %spectra.1 = bf16[8,24,256]{2,1,0:T(8,128)(2,1)S(1)} custom-call(bf16[1,256,65536]{2,1,0:T(8,128)(2,1)} %x_hbm.1, f32[4,8192]{1,0:T(4,128)} %taps_hbm.1, f32[8,8192]{1,0:T(8,128)} %constant.2.clone.dft_hbm), custom_call_target="tpu_custom_call" | custom-call | tf_op jit(solution)/shard_map/spectra/pallas_call | solution.py:325
  12.7 14.2 %all_to_all.5.own_ref = bf16[8,24,256]{2,1,0:T(8,128)(2,1)S(1)} all-to-all(bf16[8,24,256]{2,1,0:T(8,128)(2,1)S(1)} %spectra.1), channel_id=1, replica_groups={{0,2,4,6,8,10,12,14},{1,3,5,7,9,11,13,15},{16,18,20,22,24,26,28,30},{17..., dimensions={0} | all-to-all | bytes 196608 | tf_op jit(solution)/shard_map/all_to_all | solution.py:345
  26.9 0.0 collective-permute-start
  26.9 1.7 %near.1._ = f32[512,4096]{1,0:T(8,128)} custom-call(bf16[8,24,256]{2,1,0:T(8,128)(2,1)S(1)} %all_to_all.5.own_ref), custom_call_target="tpu_custom_call" | custom-call | flops 33554432 | bytes 2097152 | tf_op jit(solution)/shard_map/near/pallas_call | solution.py:280
  28.6 0.0 collective-permute-done.other_ref
  28.6 3.2 %far.1 = f32[512,4096]{1,0:T(8,128)} custom-call(bf16[8,24,256]{2,1,0:T(8,128)(2,1)S(1)} %all_to_all.5.own_ref, bf16[8,24,256]{2,1,0:T(8,128)(2,1)S(1)} %collective-permute-done.other_ref, f32[512,4096]{1,0:T(8,128)} %near.1._), custom_call_target="tpu_custom_call", output_to_operand_aliasing={{}: (2, {})} | custom-call | tf_op jit(solution)/shard_map/far/pallas_call | solution.py:295
Async XLA Ops:
  26.9 1.7 %collective-permute-start = (bf16[8,24,256]{2,1,0:T(8,128)(2,1)S(1)}, bf16[8,24,256]{2,1,0:T(8,128)(2,1)S(1)}, u32[]{:S(2)}, u32[]{:S(2)}) collective-permute-start(bf16[8,24,256]{2,1,0:T(8,128)(2,1)S(1)} %all_to_all.5.own_ref), channel_id=1, source_target_pairs={{0,1},{1,0},{2,3},{3,2},{4,5},{5,4},{6,7},{7,6},{8,9},{9,8},{10,11... | collective-permute-start | bytes 294920 | tf_op jit(solution)/shard_map/ppermute | solution.py:348
